TPU v7x, 128 devices: a whole 4x4x4 slice. The times are simulated.
128 devices in a mesh: row: 8 (over z, y_hi), col: 16 (over x, y_lo, core).
Axes of the slice: x: 4, y: 4 (y_hi: 2, y_lo: 2; y = y_hi * 2 + y_lo), z: 4, core: 2. Of those that a mesh axis runs over, the one named last changes fastest.
Arguments:
- pair: bfloat16 [768, 768, 128], P('row', 'col'), may hold values from -6 to 6
- residue_mask: int32 [768], replicated, may hold values 0 or 1
- out_ab_weight: bfloat16 [128, 512], replicated, may hold values from -0.5 to 0.5
- out_gate_weight: bfloat16 [128, 128], replicated, may hold values from -0.5 to 0.5
- out_z_weight: bfloat16 [128, 128], replicated, may hold values from -0.5 to 0.5
- in_ab_weight: bfloat16 [128, 512], replicated, may hold values from -0.5 to 0.5
- in_gate_weight: bfloat16 [128, 128], replicated, may hold values from -0.5 to 0.5
- in_z_weight: bfloat16 [128, 128], replicated, may hold values from -0.5 to 0.5
- trans_up: bfloat16 [128, 512], replicated, may hold values from -0.5 to 0.5
- trans_down: bfloat16 [512, 128], replicated, may hold values from -0.25 to 0.25
Outputs:
- updated_pair: bfloat16 [768, 768, 128], P('row', 'col')
All inputs are finite; a program needn't handle non-finite values.
Results may differ from a plain program's by a relative error of at most 0.02.
Values may be sent and summed in bfloat16 or wider, within the bound.
A program may use at most 256 MiB of HBM per device.

v0:
```python
import jax
import jax.numpy as jnp
from jax import lax
from jax.sharding import PartitionSpec as P

EPS = 1e-05


def layer_norm(values):
    values = values.astype(jnp.float32)
    center = values - jnp.mean(values, axis=-1, keepdims=True)
    return center * lax.rsqrt(jnp.mean(center * center, axis=-1, keepdims=True) + EPS)


def project_matrix(normed, weight):
    return jnp.einsum("ijc,cd->ijd", normed, weight, preferred_element_type=jnp.float32)


def gated_operand(normed, weight, pair_mask, first):
    hidden = weight.shape[1] // 4
    columns = weight[:, first * hidden : (first + 2) * hidden]
    projected = project_matrix(normed, columns)
    gated = (
        pair_mask[:, :, None] * jax.nn.sigmoid(projected[:, :, hidden:]) * projected[:, :, :hidden]
    )
    return gated.astype(jnp.bfloat16)


def finish(triangle, gating, z_weight, current):
    normed = layer_norm(triangle).astype(jnp.bfloat16)
    update = gating * project_matrix(normed, z_weight)
    return (current.astype(jnp.float32) + update).astype(jnp.bfloat16)


def body(
    pair,
    residue_mask,
    out_ab_weight,
    out_gate_weight,
    out_z_weight,
    in_ab_weight,
    in_gate_weight,
    in_z_weight,
    trans_up,
    trans_down,
):
    rows_here = pair.shape[0]
    cols_here = pair.shape[1]
    row_index = lax.axis_index("row")
    col_index = lax.axis_index("col")
    present = residue_mask.astype(jnp.float32)
    mask_rows = lax.dynamic_slice_in_dim(present, row_index * rows_here, rows_here)
    mask_cols = lax.dynamic_slice_in_dim(present, col_index * cols_here, cols_here)
    tile_mask = mask_rows[:, None] * mask_cols[None, :]
    normed = layer_norm(pair).astype(jnp.bfloat16)
    left = gated_operand(normed, out_ab_weight, tile_mask, 0)
    right = gated_operand(normed, out_ab_weight, tile_mask, 2)
    gating = jax.nn.sigmoid(project_matrix(normed, out_gate_weight))
    right_rows = lax.all_gather(right, "row", axis=0, tiled=True)
    right_all = lax.all_to_all(right_rows, "col", split_axis=0, concat_axis=1, tiled=True)
    left_piece = lax.all_gather(left, "col", axis=1, tiled=True)
    width = left_piece.shape[1]
    blocks = width // cols_here
    hidden = left_piece.shape[2]
    left_blocks = left_piece.reshape(rows_here, blocks, cols_here, hidden)
    right_blocks = right_all.reshape(cols_here, blocks, cols_here, hidden)
    sums = jnp.einsum(
        "imkh,jmkh->mijh", left_blocks, right_blocks, preferred_element_type=jnp.float32
    )
    rounded = lax.optimization_barrier(sums.astype(jnp.bfloat16)).astype(jnp.float32)
    triangle = jnp.sum(rounded, axis=0)
    updated = finish(triangle, gating, out_z_weight, pair)
    normed_in = layer_norm(updated).astype(jnp.bfloat16)
    right_in = gated_operand(normed_in, in_ab_weight, tile_mask, 2)
    gating_in = jax.nn.sigmoid(project_matrix(normed_in, in_gate_weight))
    left_in = gated_operand(normed_in, in_ab_weight, tile_mask, 0)
    left_cols = lax.all_gather(left_in, "col", axis=1, tiled=True)
    triangle_in = lax.psum_scatter(
        jnp.einsum("kih,kjh->ijh", left_cols, right_in, preferred_element_type=jnp.float32).astype(
            jnp.bfloat16
        ),
        "row",
        scatter_dimension=0,
        tiled=True,
    ).astype(jnp.float32)
    second = finish(triangle_in, gating_in, in_z_weight, updated)
    normed_out = layer_norm(second).astype(jnp.bfloat16)
    expanded = jax.nn.relu(project_matrix(normed_out, trans_up)).astype(jnp.bfloat16)
    return (second.astype(jnp.float32) + project_matrix(expanded, trans_down)).astype(jnp.bfloat16)


def solution(mesh):
    placed = (P("row", "col", None), P(), P(), P(), P(), P(), P(), P(), P(), P())
    return jax.shard_map(
        body, mesh=mesh, in_specs=placed, out_specs=P("row", "col", None), check_vma=False
    )
```

profile of v0, /device:TPU:1, one launch (start us, length us, event | category | flops | bytes accessed | tf_op | source)
XLA Modules:
  0.0 777.0 jit_solution(16842807308683282464)
XLA Ops:
  6.5 0.0 copy-start
  6.5 0.0 copy-start.1
  6.5 0.0 all-gather.4.cloned.1.call-start
  6.6 2.1 convert_reduce_fusion.4
  8.6 2.5 fusion.20
  11.1 0.0 copy-done.1
  11.2 0.0 copy-done.3
  11.2 3.8 fusion.56
  14.9 3.6 fusion.58
  18.5 0.0 copy-done.7
  18.6 0.1 dynamic_slice.6
  18.6 0.1 dynamic_slice.7
  18.7 0.1 broadcast_multiply_fusion
  18.8 5.4 fusion.42
  24.2 0.0 all-gather.4.cloned.1.call-update
  24.2 0.0 all-gather.6.cloned.1.call-start
  24.3 0.7 all-gather.6.cloned.1.call-update
  25.0 0.0 copy-start.5
  25.0 118.9 %all-gather.4.cloned.1.call-done = bf16[768,48,128]{2,1,0:T(8,128)(2,1)} async-done(((bf16[96,48,128]{2,1,0:T(8,128)(2,1)}), bf16[768,48,128]{2,1,0:T(8,128)(2,1)}) %all-gather.4.cloned.1.call-update) | async-done | bytes 9437200 | tf_op jit(solution)/shard_map/all_gather | solution.py:59
  143.9 5.6 all-to-all-start
  149.6 0.2 all-gather.8.cloned.1.call-start
  149.8 0.0 copy-done.5
  149.8 3.1 fusion.60
  152.9 182.0 %all-to-all-done = bf16[768,48,128]{2,1,0:T(8,128)(2,1)} async-done(((bf16[768,48,128]{2,1,0:T(8,128)(2,1)}), bf16[768,48,128]{2,1,0:T(8,128)(2,1)}, u32[]{:S(2)}, u32[]{:S(2)}) %all-to-all-start) | async-done | bytes 9437216 | tf_op jit(solution)/shard_map/all_to_all | solution.py:60
  334.9 26.4 %copy.62 = bf16[16,48,48,128]{2,1,3,0:T(8,128)(2,1)} copy(bf16[16,48,48,128]{3,2,1,0:T(8,128)(2,1)} %bitcast.2) | data formatting | bytes 18874368 | tf_op jit(solution)/shard_map/all_to_all | solution.py:60
  361.4 32.7 %copy.63 = bf16[96,16,48,128]{0,2,3,1:T(8,128)(2,1)} copy(bf16[96,16,48,128]{3,2,1,0:T(8,128)(2,1)} %bitcast.50) | data formatting | bytes 37748736 | tf_op jit(solution)/shard_map/reshape | solution.py:65
  394.1 26.7 %convert_bitcast_fusion = bf16[16,96,48,128]{1,2,3,0:T(8,128)(2,1)} fusion(bf16[96,16,48,128]{0,2,3,1:T(8,128)(2,1)} %copy.63, bf16[16,48,48,128]{2,1,3,0:T(8,128)(2,1)} %copy.62), kind=kOutput, calls=%fused_computation.4 | convolution fusion | flops 915406848 | bytes 47185920 | tf_op jit(solution)/shard_map/imkh,jmkh->mijh/dot_general | solution.py:67
  420.8 20.3 %convert_reduce_fusion = (f32[96,48]{0,1:T(8,128)S(1)}, f32[96,48,128]{0,1,2:T(8,128)}) fusion(bf16[16,96,48,128]{1,2,3,0:T(8,128)(2,1)} %convert_bitcast_fusion), kind=kLoop, calls=%fused_computation | loop fusion | flops 27717120 | bytes 21252096 | tf_op jit(solution)/shard_map/reduce_sum | solution.py:11
  441.1 0.1 copy.64
  441.2 0.1 copy.65
  441.3 2.4 multiply_reduce_fusion
  443.6 0.1 copy.66
  443.7 0.1 copy.67
  443.8 2.3 multiply_convert_fusion
  446.1 0.0 copy-start.9
  446.1 2.1 copy.68
  448.2 0.0 copy-done.9
  448.2 3.0 convert_reduce_fusion.3
  451.2 1.6 fusion.18
  452.8 0.0 copy-done.4
  452.8 1.4 fusion.64
  454.3 1.4 fusion.62
  455.7 2.4 fusion.27
  458.1 0.0 all-gather.8.cloned.1.call-update
  458.1 0.0 reduce-scatter.2.cloned.1.call-start
  458.2 2.1 copy.69
  460.3 107.9 %all-gather.8.cloned.1.call-done = bf16[96,768,128]{2,1,0:T(8,128)(2,1)} async-done(((bf16[96,48,128]{2,1,0:T(8,128)(2,1)}), bf16[96,768,128]{2,1,0:T(8,128)(2,1)}) %all-gather.8.cloned.1.call-update) | async-done | bytes 18874384 | tf_op jit(solution)/shard_map/all_gather | solution.py:77
  568.2 32.6 %copy.70 = bf16[96,768,128]{0,1,2:T(8,128)(2,1)} copy(bf16[96,768,128]{2,1,0:T(8,128)(2,1)} %all-gather.8.cloned.1.call-done) | data formatting | bytes 37748736 | tf_op jit(solution)/shard_map/all_gather | solution.py:77
  600.8 17.3 %convert_bitcast_fusion.1 = bf16[768,48,128]{0,1,2:T(8,128)(2,1)} fusion(bf16[96,48,128]{0,1,2:T(8,128)(2,1)} %copy.69, bf16[96,768,128]{0,1,2:T(8,128)(2,1)} %copy.70), kind=kOutput, calls=%fused_computation.6 | convolution fusion | flops 910688256 | bytes 29491200 | tf_op jit(solution)/shard_map/kih,kjh->ijh/dot_general | solution.py:79
  618.1 14.0 %copy.71 = bf16[768,48,128]{2,1,0:T(8,128)(2,1)} copy(bf16[768,48,128]{0,1,2:T(8,128)(2,1)} %convert_bitcast_fusion.1) | data formatting | bytes 18874368 | tf_op jit(solution)/shard_map/convert_element_type | solution.py:79
  632.1 0.0 reduce-scatter.2.cloned.1.call-update
  632.1 0.7 copy-done.6
  632.8 3.1 fusion.66
  635.9 120.8 %reduce-scatter.2.cloned.1.call-done = bf16[96,48,128]{2,1,0:T(8,128)(2,1)} async-done(((bf16[768,48,128]{2,1,0:T(8,128)(2,1)}), bf16[96,48,128]{2,1,0:T(8,128)(2,1)}) %reduce-scatter.2.cloned.1.call-update) | async-done | bytes 1179664 | tf_op jit(solution)/shard_map/reduce_scatter | solution.py:78
  756.7 2.0 convert_reduce_fusion.5
  758.7 2.5 fusion.22
  761.2 0.0 copy-done.10
  761.3 0.0 copy-done.2
  761.3 0.0 copy-start.8
  761.3 4.0 convert_reduce_fusion.2
  765.3 1.4 fusion.16
  766.7 0.0 copy-done
  766.7 0.0 copy-done.8
  766.7 3.7 fusion.26
  (18 shorter events, 0.1 us)
Async XLA Ops:
  6.5 760.2 %copy-start = (bf16[512,128]{1,0:T(8,128)(2,1)S(1)}, bf16[512,128]{1,0:T(8,128)(2,1)}, u32[]{:S(2)}) copy-start(bf16[512,128]{1,0:T(8,128)(2,1)} %param.19) | copy-start | bytes 393220
  6.5 4.6 copy-start.1
  6.5 4.6 copy-start.3
  6.5 137.4 %all-gather.4.cloned.1.call-start = ((), (), s32[]{:S(2)}) async-start(), calls=%async_computation.2 | async-start | bytes 10616832 | tf_op jit(solution)/shard_map/all_gather | solution.py:59
  14.9 3.6 copy-start.7
  24.2 337.2 %all-gather.6.cloned.1.call-start = ((), (), s32[]{:S(2)}) async-start(), calls=%async_computation.3 | async-start | bytes 20054016 | tf_op jit(solution)/shard_map/all_gather | solution.py:61
  25.0 124.8 %copy-start.5 = (bf16[128,128]{1,0:T(8,128)(2,1)S(1)}, bf16[128,128]{1,0:T(8,128)(2,1)}, u32[]{:S(2)}) copy-start(bf16[128,128]{1,0:T(8,128)(2,1)} %param.13) | copy-start | bytes 98308
  143.9 191.0 %all-to-all-start = ((bf16[768,48,128]{2,1,0:T(8,128)(2,1)}), bf16[768,48,128]{2,1,0:T(8,128)(2,1)}, u32[]{:S(2)}, u32[]{:S(2)}) async-start(bf16[768,48,128]{2,1,0:T(8,128)(2,1)} %all-gather.4.cloned.1.call-done), calls=%async_computation | async-start | bytes 18874368 | tf_op jit(solution)/shard_map/all_to_all | solution.py:60
  149.6 418.6 %all-gather.8.cloned.1.call-start = ((), (), s32[]{:S(2)}) async-start(), calls=%async_computation.4 | async-start | bytes 20054016 | tf_op jit(solution)/shard_map/all_gather | solution.py:77
  446.1 2.1 copy-start.9
  448.2 4.7 copy-start.4
  458.1 298.5 %reduce-scatter.2.cloned.1.call-start = ((), (), s32[]{:S(2)}) async-start(), calls=%async_computation.5 | async-start | bytes 10616832 | tf_op jit(solution)/shard_map/reduce_scatter | solution.py:78
  632.1 0.8 copy-start.6
  632.8 128.4 %copy-start.10 = (bf16[128,128]{1,0:T(8,128)(2,1)S(1)}, bf16[128,128]{1,0:T(8,128)(2,1)}, u32[]{:S(2)}) copy-start(bf16[128,128]{1,0:T(8,128)(2,1)} %param.17) | copy-start | bytes 98308
  756.7 4.6 copy-start.2
  761.3 5.5 copy-start.8
Sparse Core Ops, SparseCore 0:
  24.3 119.5 all-gather.3
  145.6 212.8 all-gather.5
  458.3 109.8 all-gather.7
  632.2 124.4 reduce-scatter.1
where the time goes:
time: 780 us; the launch traced here: 777 us
  waiting for transfers between devices  530 us (68%)
  local copies, waits for them, and re-layouts  111 us (14%)
  matrix products  71 us (9%)
  other arithmetic  45.1 us (6%)
  between operations  13.4 us (2%)
    all_to_all x1, waiting for transfers between devices, body(): lax.all_to_all(right_rows, 'col', split_axis=0, concat_axis=1, tiled=True)  182 us
    reduce_scatter x1, waiting for transfers between devices, body(): lax.psum_scatter(jnp.einsum('kih,kjh->ijh', left_cols, right_in, preferre...  121 us
    all_gather x1, waiting for transfers between devices, body(): right_rows = lax.all_gather(right, 'row', axis=0, tiled=True)  119 us
    all_gather x1, waiting for transfers between devices, body(): left_cols = lax.all_gather(left_in, 'col', axis=1, tiled=True)  108 us
    reshape x1, local copies, waits for them, and re-layouts, body(): left_blocks = left_piece.reshape(rows_here, blocks, cols_here, hidden)  32.7 us
    all_gather x1, local copies, waits for them, and re-layouts, body(): left_cols = lax.all_gather(left_in, 'col', axis=1, tiled=True)  32.6 us
    dot_general x9, matrix products, project_matrix(): jnp.einsum('ijc,cd->ijd', normed, weight, preferred_element_type=jnp.floa...  27 us
    dot_general x1, matrix products, body(): jnp.einsum('imkh,jmkh->mijh', left_blocks, right_blocks, preferred_elemen...  26.7 us
  transfers between devices with their start and end apart: 5, of which 4 were waited for; matrix products, arithmetic and copies ran while one was open for 4% of the time, Pallas kernels for 0%

commit v1 on v0

v1 whole, which is shorter than its diff:
```python
import jax
import jax.numpy as jnp
from jax import lax
from jax.sharding import PartitionSpec as P

EPS = 1e-05
AXES = ("row", "col")


def layer_norm(values, axis):
    values = values.astype(jnp.float32)
    center = values - jnp.mean(values, axis=axis, keepdims=True)
    return center * lax.rsqrt(jnp.mean(center * center, axis=axis, keepdims=True) + EPS)


def project(weight, normed):
    return lax.dot_general(
        weight, normed, (((0,), (0,)), ((), ())), preferred_element_type=jnp.float32
    )


def operands(normed, weight, mask):
    hidden = weight.shape[1] // 4
    p = project(weight, normed)
    left = mask * jax.nn.sigmoid(p[hidden : 2 * hidden]) * p[:hidden]
    right = mask * jax.nn.sigmoid(p[3 * hidden :]) * p[2 * hidden : 3 * hidden]
    return left.astype(jnp.bfloat16), right.astype(jnp.bfloat16)


def finish(triangle, gating, z_weight, current):
    normed = layer_norm(triangle, 0).astype(jnp.bfloat16)
    return (current.astype(jnp.float32) + gating * project(z_weight, normed)).astype(jnp.bfloat16)


def triangle(left, right, rows, cols, n_row, n_col, form):
    hidden = left.shape[0]
    both = jnp.stack([left, right], axis=1)
    moved = lax.all_to_all(both, AXES, 0, 0, tiled=True)
    whole = moved.reshape(n_row, n_col, 2, rows, cols).transpose(2, 0, 3, 1, 4)
    whole = whole.reshape(2, n_row * rows, n_col * cols)
    sums = jnp.einsum(form, whole[0], whole[1], preferred_element_type=jnp.float32)
    sums = sums.astype(jnp.bfloat16).reshape(n_row, rows, n_col, cols).transpose(0, 2, 1, 3)
    back = lax.all_to_all(sums.reshape(hidden, rows * cols), AXES, 0, 0, tiled=True)
    return back


def body(
    pair,
    residue_mask,
    out_ab_weight,
    out_gate_weight,
    out_z_weight,
    in_ab_weight,
    in_gate_weight,
    in_z_weight,
    trans_up,
    trans_down,
):
    n_row, n_col = lax.axis_size("row"), lax.axis_size("col")
    rows, cols, channels = pair.shape
    present = residue_mask.astype(jnp.float32)
    mask_rows = lax.dynamic_slice_in_dim(present, lax.axis_index("row") * rows, rows)
    mask_cols = lax.dynamic_slice_in_dim(present, lax.axis_index("col") * cols, cols)
    mask = (mask_rows[:, None] * mask_cols[None, :]).reshape(1, rows * cols)
    current = pair.reshape(rows * cols, channels).T
    for ab, gate, z, form in (
        (out_ab_weight, out_gate_weight, out_z_weight, "ik,jk->ij"),
        (in_ab_weight, in_gate_weight, in_z_weight, "ki,kj->ij"),
    ):
        normed = layer_norm(current, 0).astype(jnp.bfloat16)
        left, right = operands(normed, ab, mask)
        gating = jax.nn.sigmoid(project(gate, normed))
        sums = triangle(left, right, rows, cols, n_row, n_col, form)
        current = finish(sums, gating, z, current)
    normed = layer_norm(current, 0).astype(jnp.bfloat16)
    expanded = jax.nn.relu(project(trans_up, normed)).astype(jnp.bfloat16)
    out = (current.astype(jnp.float32) + project(trans_down, expanded)).astype(jnp.bfloat16)
    return out.T.reshape(rows, cols, channels)


def solution(mesh):
    placed = (P("row", "col", None), P(), P(), P(), P(), P(), P(), P(), P(), P())
    return jax.shard_map(
        body, mesh=mesh, in_specs=placed, out_specs=P("row", "col", None), check_vma=False
    )
```

time: 780 us -> 341 us (0.44)
  waiting for transfers between devices: 530 us -> 34.1 us
  blocking collectives: 0 us -> 82.4 us
  matrix products: 71 us -> 24.7 us
  local copies, waits for them, and re-layouts: 111 us -> 129 us
  between operations: 13.4 us -> 0.7 us
    all_gather x3 -> x0, waiting for transfers between devices: 227 us -> none  [the longest x1 119 us: body(): right_rows = lax.all_gather(right, 'row', axis=0, tiled=True)]
    all_to_all x1 -> x2, waiting for transfers between devices: 182 us -> 34.1 us  [triangle(): lax.all_to_all(sums.reshape(hidden, rows * cols), AXES, 0, 0, tiled=True)]
    reduce_scatter x1 -> x0, waiting for transfers between devices: 121 us -> none  [body(): lax.psum_scatter(jnp.einsum('kih,kjh->ijh', left_cols, right_in, preferre...]
    all_to_all x0 -> x2, blocking collectives: none -> 82.4 us  [triangle(): moved = lax.all_to_all(both, AXES, 0, 0, tiled=True)]
    dot_general x11 -> x9, matrix products: 71 us -> 24.7 us  [the longest x7 18.6 us: project(): lax.dot_general(weight, normed, (((0,), (0,)), ((), ())), preferred_eleme...]
    all_gather x1 -> x0, local copies, waits for them, and re-layouts: 32.6 us -> none  [body(): left_cols = lax.all_gather(left_in, 'col', axis=1, tiled=True)]
    slice x0 -> x6, local copies, waits for them, and re-layouts: none -> 28.6 us  [the longest x4 19.8 us: triangle(): whole[1]]
    unnamed x22 -> x40, local copies, waits for them, and re-layouts: 0.78 us -> 20.6 us
  transfers between devices with their start and end apart: 5 -> 2, of which waited for: 4 -> 2; matrix products, arithmetic and copies ran while one was open for 4% -> 2% of each run, Pallas kernels for 0% -> 0%
where the time goes in v1:
time: 341 us; the launch traced here: 334 us
  local copies, waits for them, and re-layouts  129 us (38%)
  blocking collectives  82.4 us (24%)
  other arithmetic  50.7 us (15%)
  waiting for transfers between devices  34.1 us (10%)
  matrix products  24.7 us (7%)
  starting transfers between devices  12 us (4%)
    all_to_all x2, blocking collectives, triangle(): moved = lax.all_to_all(both, AXES, 0, 0, tiled=True)  82.4 us
    all_to_all x2, waiting for transfers between devices, triangle(): lax.all_to_all(sums.reshape(hidden, rows * cols), AXES, 0, 0, tiled=True)  34.1 us
    unnamed x40, local copies, waits for them, and re-layouts  20.6 us
    slice x4, local copies, waits for them, and re-layouts, triangle(): whole[1]  19.8 us
    all_to_all x2, other arithmetic, triangle(): lax.all_to_all(sums.reshape(hidden, rows * cols), AXES, 0, 0, tiled=True)  18.6 us
    dot_general x7, matrix products, project(): lax.dot_general(weight, normed, (((0,), (0,)), ((), ())), preferred_eleme...  18.6 us
    reshape x2, local copies, waits for them, and re-layouts, triangle(): whole = moved.reshape(n_row, n_col, 2, rows, cols).transpose(2, 0, 3, 1, 4)  17 us
    all_to_all x3, local copies, waits for them, and re-layouts, triangle(): lax.all_to_all(sums.reshape(hidden, rows * cols), AXES, 0, 0, tiled=True)  16.9 us
  transfers between devices with their start and end apart: 2, of which 2 were waited for; matrix products, arithmetic and copies ran while one was open for 2% of the time, Pallas kernels for 0%

profile of v1, /device:TPU:1, one launch (start us, length us, event | category | flops | bytes accessed | tf_op | source)
XLA Modules:
  0.0 334.0 jit_solution(4998929535032526306)
XLA Ops:
  0.0 0.8 convert_element_type.104
  1.1 2.0 convert_reduce_fusion
  3.2 2.7 multiply_reduce_fusion.2
  5.9 2.5 multiply_convert_fusion.2
  8.4 1.0 copy-done.6
  9.4 1.4 convolution_bitcast_fusion.1
  10.8 2.2 fusion.41
  13.0 0.2 pad_maximum_fusion
  13.2 4.6 %copy.21 = bf16[128,2,4608]{2,1,0:T(2,128)(2,1)} copy(bf16[128,2,4608]{0,2,1:T(8,128)(2,1)S(1)} %pad_maximum_fusion) | data formatting | bytes 4718592 | tf_op jit(solution)/shard_map/stack | solution.py:37
  17.9 44.7 %all_to_all.30 = bf16[128,2,4608]{2,1,0:T(2,128)(2,1)S(1)} all-to-all(bf16[128,2,4608]{2,1,0:T(2,128)(2,1)} %copy.21), channel_id=1, replica_groups=mesh['row'=8,'col'=16] {'row','col'}, dimensions={0} | all-to-all | bytes 4718592 | tf_op jit(solution)/shard_map/all_to_all | solution.py:38
  62.6 0.2 copy.22
  62.8 7.6 %reshape.119 = bf16[8,16,2,96,48]{4,3,1,0,2:T(8,128)(2,1)} reshape(bf16[128,2,4608]{2,0,1:T(8,128)(2,1)S(1)} %copy.22) | data formatting | bytes 4718592 | tf_op jit(solution)/shard_map/reshape | solution.py:39
  70.4 5.9 %fusion.47 = (bf16[1,8,96,16,48]{4,2,3,1,0:T(8,128)(2,1)S(1)}, bf16[1,8,96,16,48]{4,2,3,1,0:T(8,128)(2,1)}) fusion(bf16[2,8,96,16,48]{4,2,3,1,0:T(8,128)(2,1)} %bitcast.84), kind=kLoop, calls=%fused_computation.92 | loop fusion | bytes 4718592 | tf_op jit(solution)/shard_map/slice | solution.py:41
  76.3 4.4 %copy.23 = bf16[1,8,96,16,48]{2,1,4,3,0:T(8,128)(2,1)} copy(bf16[1,8,96,16,48]{4,2,3,1,0:T(8,128)(2,1)} %get-tuple-element.12) | data formatting | bytes 2359296 | tf_op jit(solution)/shard_map/slice | solution.py:41
  80.7 3.8 %squeeze.12 = bf16[768,768]{0,1:T(8,128)(2,1)} reshape(bf16[1,8,96,16,48]{2,1,4,3,0:T(8,128)(2,1)} %copy.23) | data formatting | bytes 2359296 | tf_op jit(solution)/shard_map/squeeze | solution.py:41
  84.5 2.6 copy.24
  87.1 3.9 %squeeze.13 = bf16[768,768]{0,1:T(8,128)(2,1)} reshape(bf16[1,8,96,16,48]{2,1,4,3,0:T(8,128)(2,1)} %copy.24) | data formatting | bytes 2359296 | tf_op jit(solution)/shard_map/squeeze | solution.py:41
  91.0 2.4 convolution_convert_fusion.1
  93.4 0.6 copy.25
  94.1 2.6 reshape.120
  96.7 3.3 copy.26
  100.0 5.5 %all_to_all.24 = bf16[128,1,4608]{2,1,0:T(2,128)(2,1)} reshape(bf16[8,16,96,48]{3,2,1,0:T(8,128)(2,1)S(1)} %copy.26) | data formatting | bytes 2359296 | tf_op jit(solution)/shard_map/all_to_all | solution.py:43
  105.5 0.5 broadcast.176
  106.0 8.8 %reduce.9 = bf16[128,4608]{1,0:T(8,128)(2,1)S(1)} reduce(bf16[128,1,4608]{2,1,0:T(2,128)(2,1)} %all_to_all.24, bf16[]{:T(256)} %broadcast.176), dimensions={1}, to_apply=%all_to_all.24.reduce_sub_computation | reduce | bytes 2359298 | tf_op jit(solution)/shard_map/all_to_all | solution.py:43
  114.9 1.2 reshape.125
  116.0 5.9 %all-to-all-start.1 = ((bf16[128,2,2304]{2,1,0:T(2,128)(2,1)}), bf16[128,2,2304]{2,1,0:T(2,128)(2,1)}, u32[]{:S(2)}, u32[]{:S(2)}) async-start(bf16[128,2,2304]{2,1,0:T(2,128)(2,1)} %reshape.125), calls=%async_computation.1 | async-start | bytes 2359296 | tf_op jit(solution)/shard_map/all_to_all | solution.py:43
  121.9 2.2 fusion.6
  124.1 18.1 %all-to-all-done.1 = bf16[128,2,2304]{2,1,0:T(2,128)(2,1)} async-done(((bf16[128,2,2304]{2,1,0:T(2,128)(2,1)}), bf16[128,2,2304]{2,1,0:T(2,128)(2,1)}, u32[]{:S(2)}, u32[]{:S(2)}) %all-to-all-start.1) | async-done | bytes 1179680 | tf_op jit(solution)/shard_map/all_to_all | solution.py:43
  142.2 6.8 %reshape.126 = bf16[128,1,4608]{2,1,0:T(2,128)(2,1)S(1)} reshape(bf16[128,2,2304]{2,1,0:T(2,128)(2,1)} %all-to-all-done.1) | data formatting | bytes 2359296
  149.0 2.4 convert_element_type.108
  151.5 2.4 convert_reduce_fusion.2
  153.8 0.3 multiply_reduce_fusion.4
  154.2 1.1 fusion.48
  155.3 2.7 multiply_reduce_fusion.1
  158.0 1.4 convolution_bitcast_fusion
  159.5 2.2 fusion.43
  161.7 1.6 pad_maximum_fusion.1
  163.3 6.9 %copy.28 = bf16[128,2,4608]{2,1,0:T(2,128)(2,1)} copy(bf16[128,2,4608]{0,2,1:T(8,128)(2,1)} %pad_maximum_fusion.1) | data formatting | bytes 4718592 | tf_op jit(solution)/shard_map/stack | solution.py:37
  170.1 37.7 %all_to_all.31 = bf16[128,2,4608]{2,1,0:T(2,128)(2,1)S(1)} all-to-all(bf16[128,2,4608]{2,1,0:T(2,128)(2,1)} %copy.28), channel_id=1, replica_groups=mesh['row'=8,'col'=16] {'row','col'}, dimensions={0} | all-to-all | bytes 4718592 | tf_op jit(solution)/shard_map/all_to_all | solution.py:38
  207.8 1.6 copy.29
  209.5 9.4 %reshape.121 = bf16[8,16,2,96,48]{4,3,1,0,2:T(8,128)(2,1)} reshape(bf16[128,2,4608]{2,0,1:T(8,128)(2,1)} %copy.29) | data formatting | bytes 4718592 | tf_op jit(solution)/shard_map/reshape | solution.py:39
  218.8 6.9 %fusion.46 = (bf16[1,8,96,16,48]{4,2,3,1,0:T(8,128)(2,1)}, bf16[1,8,96,16,48]{4,2,3,1,0:T(8,128)(2,1)}) fusion(bf16[2,8,96,16,48]{4,2,3,1,0:T(8,128)(2,1)} %bitcast.85), kind=kLoop, calls=%fused_computation.91 | loop fusion | bytes 4718592 | tf_op jit(solution)/shard_map/slice | solution.py:41
  225.7 4.4 %copy.30 = bf16[1,8,96,16,48]{2,1,4,3,0:T(8,128)(2,1)} copy(bf16[1,8,96,16,48]{4,2,3,1,0:T(8,128)(2,1)} %get-tuple-element.10) | data formatting | bytes 2359296 | tf_op jit(solution)/shard_map/slice | solution.py:41
  230.1 3.8 %squeeze.14 = bf16[768,768]{0,1:T(8,128)(2,1)} reshape(bf16[1,8,96,16,48]{2,1,4,3,0:T(8,128)(2,1)} %copy.30) | data formatting | bytes 2359296 | tf_op jit(solution)/shard_map/squeeze | solution.py:41
  233.9 4.4 %copy.31 = bf16[1,8,96,16,48]{2,1,4,3,0:T(8,128)(2,1)} copy(bf16[1,8,96,16,48]{4,2,3,1,0:T(8,128)(2,1)} %get-tuple-element.9) | data formatting | bytes 2359296 | tf_op jit(solution)/shard_map/slice | solution.py:41
  238.4 3.8 %squeeze.15 = bf16[768,768]{0,1:T(8,128)(2,1)} reshape(bf16[1,8,96,16,48]{2,1,4,3,0:T(8,128)(2,1)} %copy.31) | data formatting | bytes 2359296 | tf_op jit(solution)/shard_map/squeeze | solution.py:41
  242.2 3.7 %convolution_convert_fusion = bf16[768,768]{1,0:T(8,128)(2,1)} fusion(bf16[768,768]{0,1:T(8,128)(2,1)} %squeeze.14, bf16[768,768]{0,1:T(8,128)(2,1)} %squeeze.15), kind=kOutput, calls=%fused_computation.65 | convolution fusion | flops 906559488 | bytes 3538944 | tf_op jit(solution)/shard_map/ki,kj->ij/dot_general | solution.py:41
  245.9 2.4 copy.32
  248.3 4.0 %reshape.122 = bf16[8,96,16,48]{1,0,3,2:T(8,128)(2,1)} reshape(bf16[768,768]{0,1:T(8,128)(2,1)} %copy.32) | data formatting | bytes 2359296 | tf_op jit(solution)/shard_map/reshape | solution.py:42
  252.3 4.5 %copy.33 = bf16[8,16,96,48]{3,2,1,0:T(8,128)(2,1)} copy(bf16[8,16,96,48]{2,0,3,1:T(8,128)(2,1)} %bitcast.88) | data formatting | bytes 2359296 | tf_op jit(solution)/shard_map/transpose | solution.py:42
  256.8 10.8 %all_to_all.25 = bf16[128,1,4608]{2,1,0:T(2,128)(2,1)} reshape(bf16[8,16,96,48]{3,2,1,0:T(8,128)(2,1)} %copy.33) | data formatting | bytes 2359296 | tf_op jit(solution)/shard_map/all_to_all | solution.py:43
  267.6 9.8 %reduce.10 = bf16[128,4608]{1,0:T(8,128)(2,1)} reduce(bf16[128,1,4608]{2,1,0:T(2,128)(2,1)} %all_to_all.25, bf16[]{:T(256)} %broadcast.176), dimensions={1}, to_apply=%all_to_all.25.reduce_sub_computation | reduce | bytes 2359298 | tf_op jit(solution)/shard_map/all_to_all | solution.py:43
  277.4 2.2 reshape.127
  279.6 6.1 %all-to-all-start.3 = ((bf16[128,2,2304]{2,1,0:T(2,128)(2,1)}), bf16[128,2,2304]{2,1,0:T(2,128)(2,1)}, u32[]{:S(2)}, u32[]{:S(2)}) async-start(bf16[128,2,2304]{2,1,0:T(2,128)(2,1)} %reshape.127), calls=%async_computation.3 | async-start | bytes 2359296 | tf_op jit(solution)/shard_map/all_to_all | solution.py:43
  285.8 4.4 %fusion.7 = f32[4608,128]{1,0:T(8,128)} fusion(bf16[128,128]{1,0:T(8,128)(2,1)S(1)} %copy-done.17, f32[4608,128]{1,0:T(8,128)S(1)} %get-tuple-element.14, f32[4608]{0:T(1024)S(1)} %add_rsqrt_fusion.2, f32[4608]{0:T(1024)S(1)} %broadcast_multiply_fusion.4), kind=kOutput, calls=%fused_computation.15 | convolution fusion | flops 154533888 | bytes 4788224 | tf_op jit(solution)/shard_map/dot_general | solution.py:17
  290.2 16.0 %all-to-all-done.3 = bf16[128,2,2304]{2,1,0:T(2,128)(2,1)} async-done(((bf16[128,2,2304]{2,1,0:T(2,128)(2,1)}), bf16[128,2,2304]{2,1,0:T(2,128)(2,1)}, u32[]{:S(2)}, u32[]{:S(2)}) %all-to-all-start.3) | async-done | bytes 1179680 | tf_op jit(solution)/shard_map/all_to_all | solution.py:43
  306.1 8.0 %reshape.128 = bf16[128,1,4608]{2,1,0:T(2,128)(2,1)} reshape(bf16[128,2,2304]{2,1,0:T(2,128)(2,1)} %all-to-all-done.3) | data formatting | bytes 2359296
  314.1 4.2 %convert_element_type.119 = f32[128,1,4608]{2,1,0:T(1,128)S(1)} convert(bf16[128,1,4608]{2,1,0:T(2,128)(2,1)} %reshape.128) | non-fusion elementwise | flops 589824 | bytes 3538944 | tf_op jit(solution)/shard_map/convert_element_type | solution.py:11
  318.4 2.8 convert_reduce_fusion.1
  321.2 0.3 multiply_reduce_fusion.3
  321.5 1.1 fusion.49
  322.7 1.4 copy-done.5
  324.1 2.7 multiply_reduce_fusion
  326.8 7.0 %fusion.8 = bf16[4608,128]{1,0:T(8,128)(2,1)} fusion(f32[4608,128]{1,0:T(8,128)} %copy-done.5, bf16[512,128]{1,0:T(8,128)(2,1)S(1)} %copy-done.14, bf16[128,512]{1,0:T(8,128)(2,1)S(1)} %copy-done.15, f32[4608]{0:T(1024)S(1)} %add_rsqrt_fusion, f32[4608]{0:T(1024)S(1)} %broadcast_multiply_fusion.2), kind=kOutput, calls=%fused_computation.16 | convolution fusion | flops 1215627264 | bytes 3837952 | tf_op jit(solution)/shard_map/dot_general | solution.py:17
  (49 shorter events, 0.6 us)
Async XLA Ops:
  0.0 9.4 %copy-start = (bf16[128,512]{1,0:T(8,128)(2,1)S(1)}, bf16[128,512]{1,0:T(8,128)(2,1)}, u32[]{:S(2)}) copy-start(bf16[128,512]{1,0:T(8,128)(2,1)} %param.12) | copy-start | bytes 393220
  0.0 3.2 copy-start.3
  8.4 1.0 copy-start.6
  87.1 3.9 %copy-start.10 = (bf16[768,768]{0,1:T(8,128)(2,1)S(1)}, bf16[768,768]{0,1:T(8,128)(2,1)}, u32[]{:S(2)}) copy-start(bf16[768,768]{0,1:T(8,128)(2,1)} %squeeze.12) | copy-start | bytes 3538948
  114.8 7.0 %copy-start.7 = (bf16[4608,128]{1,0:T(8,128)(2,1)S(1)}, bf16[4608,128]{1,0:T(8,128)(2,1)}, u32[]{:S(2)}) copy-start(bf16[4608,128]{1,0:T(8,128)(2,1)} %copy-done.6) | copy-start | bytes 3538948
  114.9 7.0 %copy-start.16 = (bf16[128,128]{1,0:T(8,128)(2,1)S(1)}, bf16[128,128]{1,0:T(8,128)(2,1)}, u32[]{:S(2)}) copy-start(bf16[128,128]{1,0:T(8,128)(2,1)} %param.13) | copy-start | bytes 98308
  116.0 26.2 %all-to-all-start.1 = ((bf16[128,2,2304]{2,1,0:T(2,128)(2,1)}), bf16[128,2,2304]{2,1,0:T(2,128)(2,1)}, u32[]{:S(2)}, u32[]{:S(2)}) async-start(bf16[128,2,2304]{2,1,0:T(2,128)(2,1)} %reshape.125), calls=%async_computation.1 | async-start | bytes 2359296 | tf_op jit(solution)/shard_map/all_to_all | solution.py:43
  151.4 2.7 copy-start.4
  151.5 2.7 copy-start.9
  151.5 2.7 copy-start.12
  155.2 2.8 copy-start.11
  277.4 8.4 %copy-start.17 = (bf16[128,128]{1,0:T(8,128)(2,1)S(1)}, bf16[128,128]{1,0:T(8,128)(2,1)}, u32[]{:S(2)}) copy-start(bf16[128,128]{1,0:T(8,128)(2,1)} %param.16) | copy-start | bytes 98308
  279.6 26.5 %all-to-all-start.3 = ((bf16[128,2,2304]{2,1,0:T(2,128)(2,1)}), bf16[128,2,2304]{2,1,0:T(2,128)(2,1)}, u32[]{:S(2)}, u32[]{:S(2)}) async-start(bf16[128,2,2304]{2,1,0:T(2,128)(2,1)} %reshape.127), calls=%async_computation.3 | async-start | bytes 2359296 | tf_op jit(solution)/shard_map/all_to_all | solution.py:43
  314.1 4.2 %copy-start.2 = (bf16[128,1,4608]{2,1,0:T(2,128)(2,1)S(1)}, bf16[128,1,4608]{2,1,0:T(2,128)(2,1)}, u32[]{:S(2)}) copy-start(bf16[128,1,4608]{2,1,0:T(2,128)(2,1)} %reshape.128) | copy-start | bytes 3538948
  318.4 3.1 copy-start.8
  318.4 3.1 copy-start.13
  322.7 1.4 copy-start.5
  322.7 4.1 %copy-start.14 = (bf16[512,128]{1,0:T(8,128)(2,1)S(1)}, bf16[512,128]{1,0:T(8,128)(2,1)}, u32[]{:S(2)}) copy-start(bf16[512,128]{1,0:T(8,128)(2,1)} %param.19) | copy-start | bytes 393220
  322.7 4.1 %copy-start.15 = (bf16[128,512]{1,0:T(8,128)(2,1)S(1)}, bf16[128,512]{1,0:T(8,128)(2,1)}, u32[]{:S(2)}) copy-start(bf16[128,512]{1,0:T(8,128)(2,1)} %param.18) | copy-start | bytes 393220
  326.8 7.1 %copy-start.1 = (bf16[128,512]{1,0:T(8,128)(2,1)S(1)}, bf16[128,512]{1,0:T(8,128)(2,1)}, u32[]{:S(2)}) copy-start(bf16[128,512]{1,0:T(8,128)(2,1)} %param.12) | copy-start | bytes 393220

commit v2 on v1

v2 whole, which is shorter than its diff:
```python
import functools

import jax
import jax.numpy as jnp
from jax import lax
from jax.experimental import pallas as pl
from jax.experimental.pallas import tpu as pltpu
from jax.sharding import PartitionSpec as P

EPS = 1e-05
AXES = ("row", "col")
LANES = 128
SUB = 8
RUN = 16
GROUP = 4
BF16 = jnp.bfloat16
F32 = jnp.float32


def norm(x):
    center = x - jnp.mean(x, axis=0, keepdims=True)
    return center * lax.rsqrt(jnp.mean(center * center, axis=0, keepdims=True) + EPS)


def sigmoid(x):
    return 0.5 * jnp.tanh(0.5 * x) + 0.5


def dot(a, b):
    return jnp.dot(a, b, preferred_element_type=F32)


def turned(w_ref):
    return w_ref[...].astype(F32).T.astype(BF16)


def emit_operands(current, ab, gate, mask, chunk, chunks, flat, gating_ref):
    normed = norm(current).astype(BF16)
    hidden = ab.shape[0] // 4
    width = current.shape[1]
    p = dot(ab, normed)
    left = mask * sigmoid(p[hidden : 2 * hidden]) * p[:hidden]
    right = mask * sigmoid(p[3 * hidden :]) * p[2 * hidden : 3 * hidden]
    for j in range(width // LANES):
        lanes = slice(j * LANES, (j + 1) * LANES)
        flat[pl.ds(chunk + j, hidden, stride=2 * chunks), :] = left[:, lanes]
        flat[pl.ds(chunks + chunk + j, hidden, stride=2 * chunks), :] = right[:, lanes]
    here = pl.ds(pl.multiple_of(chunk * LANES, LANES), width)
    gating_ref[:, here] = sigmoid(dot(gate, normed))


def pack(flat, out_ref):
    n, rows = out_ref.shape[0], out_ref.shape[1]

    def step(i, _):
        out_ref[i] = flat[pl.ds(pl.multiple_of(i * rows, 4), rows), :].astype(out_ref.dtype)
        return 0

    lax.fori_loop(0, n, step, 0, unroll=4)


def unpack(in_ref, flat):
    n, rows = in_ref.shape[0], in_ref.shape[1]

    def step(i, _):
        flat[pl.ds(pl.multiple_of(i * rows, 4), rows), :] = in_ref[i].astype(F32)
        return 0

    lax.fori_loop(0, n, step, 0, unroll=4)


def group_mask(mask_ref, chunk):
    rows = [mask_ref[pl.ds(chunk + j, 1), :] for j in range(GROUP)]
    return jnp.concatenate(rows, axis=1)


def first_kernel(x_ref, mask_ref, ab_ref, gate_ref, out_ref, gating_ref, current_ref, flat):
    rows, cols, channels = x_ref.shape
    n_a, n_b = rows // SUB, cols // RUN
    chunks = n_a * n_b
    ab, gate = turned(ab_ref), turned(gate_ref)
    per = n_a // GROUP

    def step(g, _):
        b = g // per
        a = g % per
        block = x_ref[
            pl.ds(pl.multiple_of(a * GROUP * SUB, SUB), GROUP * SUB),
            pl.ds(pl.multiple_of(b * RUN, RUN), RUN),
            :,
        ]
        current = block.astype(F32).reshape(GROUP * LANES, channels).T
        here = pl.ds(pl.multiple_of(g * GROUP * LANES, LANES), GROUP * LANES)
        current_ref[:, here] = current.astype(BF16)
        chunk = g * GROUP
        emit_operands(
            current, ab, gate, group_mask(mask_ref, chunk), chunk, chunks, flat, gating_ref
        )
        return 0

    lax.fori_loop(0, chunks // GROUP, step, 0)
    pack(flat, out_ref)


def finish(flat_in, chunk, chunks, z, gating, current):
    channels = current.shape[0]
    triangle = jnp.concatenate(
        [flat_in[pl.ds(chunk + j, channels, stride=chunks), :] for j in range(GROUP)], axis=1
    )
    update = gating * dot(z, norm(triangle).astype(BF16))
    return (current.astype(F32) + update).astype(BF16)


def middle_kernel(
    t_ref, current_in, gating_in, mask_ref, z_ref, ab_ref, gate_ref,
    out_ref, gating_ref, current_ref, flat_in, flat,
):
    chunks = t_ref.shape[1]
    z, ab, gate = turned(z_ref), turned(ab_ref), turned(gate_ref)
    unpack(t_ref, flat_in)

    def step(g, _):
        chunk = g * GROUP
        here = pl.ds(pl.multiple_of(chunk * LANES, LANES), GROUP * LANES)
        current = finish(flat_in, chunk, chunks, z, gating_in[:, here], current_in[:, here])
        current_ref[:, here] = current
        emit_operands(
            current.astype(F32), ab, gate, group_mask(mask_ref, chunk), chunk, chunks, flat,
            gating_ref,
        )
        return 0

    lax.fori_loop(0, chunks // GROUP, step, 0)
    pack(flat, out_ref)


def last_kernel(
    t_ref, current_in, gating_in, z_ref, up_ref, down_ref, out_ref, flat_in
):
    chunks = t_ref.shape[1]
    rows, cols, channels = out_ref.shape
    per = (rows // SUB) // GROUP
    z, up, down = turned(z_ref), turned(up_ref), turned(down_ref)
    unpack(t_ref, flat_in)

    def step(g, _):
        chunk = g * GROUP
        here = pl.ds(pl.multiple_of(chunk * LANES, LANES), GROUP * LANES)
        current = finish(flat_in, chunk, chunks, z, gating_in[:, here], current_in[:, here])
        current = current.astype(F32)
        expanded = jnp.maximum(dot(up, norm(current).astype(BF16)), 0.0).astype(BF16)
        result = current + dot(down, expanded)
        b = g // per
        a = g % per
        out_ref[
            pl.ds(pl.multiple_of(a * GROUP * SUB, SUB), GROUP * SUB),
            pl.ds(pl.multiple_of(b * RUN, RUN), RUN),
            :,
        ] = result.T.reshape(GROUP * SUB, RUN, channels).astype(out_ref.dtype)
        return 0

    lax.fori_loop(0, chunks // GROUP, step, 0)


def exchange(parts):
    group = lax.broadcasted_iota(jnp.int32, parts[0].shape, 1) // RUN
    parts = list(parts)
    for bit in (1, 2, 4):
        chosen = (group // bit) % 2 == 1
        for i in range(8):
            if i & bit:
                continue
            low, high = parts[i], parts[i + bit]
            parts[i] = jnp.where(chosen, pltpu.roll(high, RUN * bit, 1), low)
            parts[i + bit] = jnp.where(chosen, high, pltpu.roll(low, LANES - RUN * bit, 1))
    return parts


def triangle_kernel(n_row, n_col, n_a, n_b, outgoing, in_ref, out_ref, flat, mats, sums, flat_out):
    chunks = n_a * n_b
    size = n_row * n_a * SUB
    tile = n_row * n_a
    unpack(in_ref, flat)

    def place(a, parity, b, a_lo):
        t = a // (n_a // 2)
        rest = a % (n_a // 2)
        return t * (n_b * LANES) + (rest // 2) * LANES + (rest % 2) * SUB + a_lo

    for operand in range(2):
        scatter = outgoing and operand == 1
        for parity in range(2):
            for b in range(n_b):
                column = (parity * n_b + b) * LANES

                def step(i, _, operand=operand, scatter=scatter, parity=parity, b=b, column=column):
                    halves = []
                    for half in range(2):
                        a = i * 2 + half
                        parts = [
                            flat[
                                pl.ds(
                                    (2 * c + parity) * 2 * chunks + operand * chunks + b * n_a + a,
                                    n_row,
                                    stride=n_col * 2 * chunks,
                                ),
                                :,
                            ]
                            for c in range(8)
                        ]
                        halves.append(exchange(parts))
                    for a_lo in range(8):
                        if scatter:
                            for half in range(2):
                                start = place(i * 2 + half, parity, b, a_lo)
                                sums[column // LANES, pl.ds(start, n_row, stride=RUN), :] = (
                                    halves[half][a_lo]
                                )
                        else:
                            both = jnp.concatenate([halves[0][a_lo], halves[1][a_lo]], axis=0)
                            mats[
                                operand,
                                pl.ds(pl.multiple_of(a_lo * tile + i * 16, 16), 16),
                                column : column + LANES,
                            ] = both.astype(BF16)
                    return 0

                lax.fori_loop(0, n_a // 2, step, 0)
        if scatter:
            for n in range(size // LANES):
                mats[operand, :, n * LANES : (n + 1) * LANES] = sums[n].astype(BF16)
    width = 2 * LANES
    for n in range(size // width):
        here = slice(n * width, (n + 1) * width)
        if outgoing:
            form, right = (((1,), (1,)), ((), ())), mats[1, here, :]
        else:
            form, right = (((0,), (0,)), ((), ())), mats[1, :, here]
        total = lax.dot_general(mats[0], right, form, preferred_element_type=F32)
        for j in range(2):
            sums[2 * n + j] = total[:, j * LANES : (j + 1) * LANES]
    for parity in range(2):
        for b in range(n_b):
            column = (parity * n_b + b) * LANES

            def leave(a, _, parity=parity, b=b, column=column):
                parts = []
                for a_lo in range(8):
                    if outgoing:
                        rows = pl.ds(pl.multiple_of(a_lo * tile + a * 8, 8), n_row)
                    else:
                        rows = pl.ds(place(a, parity, b, a_lo), n_row, stride=RUN)
                    parts.append(sums[column // LANES, rows, :])
                for c, part in enumerate(exchange(parts)):
                    flat_out[
                        pl.ds(
                            (2 * c + parity) * chunks + b * n_a + a, n_row, stride=n_col * chunks
                        ),
                        :,
                    ] = part
                return 0

            lax.fori_loop(0, n_a, leave, 0)
    pack(flat_out, out_ref)


def call(kernel, outs, scratch, *args):
    vmem = pl.BlockSpec(memory_space=pltpu.VMEM)
    many = isinstance(outs, (list, tuple))
    return pl.pallas_call(
        kernel,
        out_shape=outs,
        in_specs=[vmem] * len(args),
        out_specs=[vmem] * len(outs) if many else vmem,
        scratch_shapes=scratch,
        compiler_params=pltpu.CompilerParams(vmem_limit_bytes=56 << 20),
    )(*args)


def body(
    pair,
    residue_mask,
    out_ab_weight,
    out_gate_weight,
    out_z_weight,
    in_ab_weight,
    in_gate_weight,
    in_z_weight,
    trans_up,
    trans_down,
):
    n_row, n_col = lax.axis_size("row"), lax.axis_size("col")
    rows, cols, channels = pair.shape
    hidden = out_z_weight.shape[0]
    n_a, n_b = rows // SUB, cols // RUN
    chunks = n_a * n_b
    size = n_row * rows
    present = residue_mask.astype(F32)
    mask_rows = lax.dynamic_slice_in_dim(present, lax.axis_index("row") * rows, rows)
    mask_cols = lax.dynamic_slice_in_dim(present, lax.axis_index("col") * cols, cols)
    mask = (
        mask_rows.reshape(1, n_a, SUB, 1) * mask_cols.reshape(n_b, 1, 1, RUN)
    ).reshape(chunks, LANES)

    shape = jax.ShapeDtypeStruct
    operand_outs = [
        shape((hidden, 2 * chunks, LANES), BF16),
        shape((channels, chunks * LANES), F32),
        shape((channels, chunks * LANES), BF16),
    ]
    flat_two = pltpu.VMEM((hidden * 2 * chunks, LANES), F32)
    flat_one = pltpu.VMEM((hidden * chunks, LANES), F32)

    def move(x):
        return lax.all_to_all(x, AXES, 0, 0, tiled=True)

    def triangle(both, outgoing):
        return move(
            call(
                functools.partial(triangle_kernel, n_row, n_col, n_a, n_b, outgoing),
                shape((n_row * n_col, chunks, LANES), BF16),
                [flat_two, pltpu.VMEM((2, size, size), BF16), pltpu.VMEM((size // LANES, size, LANES), F32), flat_one],
                move(both),
            )
        )

    both, gating, current = call(
        first_kernel, operand_outs, [flat_two], pair, mask, out_ab_weight, out_gate_weight
    )
    sums = triangle(both, True)
    both, gating, current = call(
        middle_kernel, operand_outs, [flat_one, flat_two],
        sums, current, gating, mask, out_z_weight, in_ab_weight, in_gate_weight,
    )
    sums = triangle(both, False)
    return call(
        last_kernel, shape(pair.shape, pair.dtype), [flat_one],
        sums, current, gating, in_z_weight, trans_up, trans_down,
    )


def solution(mesh):
    placed = (P("row", "col", None), P(), P(), P(), P(), P(), P(), P(), P(), P())
    return jax.shard_map(
        body, mesh=mesh, in_specs=placed, out_specs=P("row", "col", None), check_vma=False
    )
```

time: 341 us -> 252 us (0.74); the launches traced: 334 us -> 251 us
  local copies, waits for them, and re-layouts: 129 us -> 1.01 us
  Pallas kernels: 0 us -> 111 us
  blocking collectives: 82.4 us -> 138 us
  other arithmetic: 50.7 us -> 0.78 us
  waiting for transfers between devices: 34.1 us -> 0 us
  matrix products: 24.7 us -> 0 us
  starting transfers between devices: 12 us -> 0 us
    pallas_call x0 -> x5, Pallas kernels: none -> 111 us  [call(): pl.pallas_call(kernel, out_shape=outs, in_specs=[vmem] * len(args), out_s...]
    all_to_all x2 -> x4, blocking collectives: 82.4 us -> 138 us  [move(): return lax.all_to_all(x, AXES, 0, 0, tiled=True)]
    all_to_all x2 -> x0, waiting for transfers between devices: 34.1 us -> none  [triangle(): lax.all_to_all(sums.reshape(hidden, rows * cols), AXES, 0, 0, tiled=True)]
    slice x6 -> x0, local copies, waits for them, and re-layouts: 28.6 us -> none  [the longest x4 19.8 us: triangle(): whole[1]]
    dot_general x9 -> x0, matrix products: 24.7 us -> none  [the longest x7 18.6 us: project(): lax.dot_general(weight, normed, (((0,), (0,)), ((), ())), preferred_eleme...]
    reshape x4 -> x0, local copies, waits for them, and re-layouts: 23.6 us -> none  [the longest x2 17 us: triangle(): whole = moved.reshape(n_row, n_col, 2, rows, cols).transpose(2, 0, 3, 1, 4)]
    unnamed x40 -> x0, local copies, waits for them, and re-layouts: 20.6 us -> none
    all_to_all x5 -> x0, local copies, waits for them, and re-layouts: 18.8 us -> none  [the longest x3 16.9 us: triangle(): lax.all_to_all(sums.reshape(hidden, rows * cols), AXES, 0, 0, tiled=True)]
  transfers between devices with their start and end apart: 2 -> 0, of which waited for: 2 -> 0; matrix products, arithmetic and copies ran while one was open for 2% -> 0% of each run, Pallas kernels for 0% -> 0%
where the time goes in v2:
time: 252 us; the launch traced here: 251 us
  blocking collectives  138 us (55%)
  Pallas kernels  111 us (44%)
    all_to_all x4, blocking collectives, move(): return lax.all_to_all(x, AXES, 0, 0, tiled=True)  138 us
    pallas_call x5, Pallas kernels, call(): pl.pallas_call(kernel, out_shape=outs, in_specs=[vmem] * len(args), out_s...  111 us

profile of v2, /device:TPU:1, one launch (start us, length us, event | category | flops | bytes accessed | tf_op | source)
XLA Modules:
  0.0 251.1 jit_solution(12272030907405936708)
XLA Ops:
  0.0 0.7 convert_element_type.3
  0.7 0.1 dynamic_slice.7
  0.8 0.1 dynamic_slice.6
  0.8 0.1 mul.31
  0.9 0.1 mul.28
  1.0 0.1 broadcast_multiply_fusion
  1.1 0.7 mul.34.mask_ref
  1.8 9.2 %shard_map.100 = (bf16[128,72,128]{2,1,0:T(8,128)(2,1)}, f32[128,4608]{1,0:T(8,128)}, bf16[128,4608]{1,0:T(8,128)(2,1)}) custom-call(bf16[96,48,128]{2,1,0:T(8,128)(2,1)} %x_ref.1, f32[36,128]{1,0:T(8,128)} %mul.34.mask_ref, bf16[128,512]{1,0:T(8,128)(2,1)} %ab_ref.2, bf16[128,128]{1,0:T(8,128)(2,1)} %gate_ref.2), custom_call_target="tpu_custom_call" | custom-call | tf_op jit(solution)/shard_map/pallas_call | solution.py:270
  11.0 44.3 %all_to_all.20.in_ref = bf16[128,72,128]{2,1,0:T(8,128)(2,1)} all-to-all(bf16[128,72,128]{2,1,0:T(8,128)(2,1)} %get-tuple-element.11), channel_id=1, replica_groups=mesh['row'=8,'col'=16] {'row','col'}, dimensions={0} | all-to-all | bytes 4718592 | tf_op jit(solution)/shard_map/all_to_all | solution.py:315
  55.3 38.4 %shard_map.101 = bf16[128,36,128]{2,1,0:T(8,128)(2,1)} custom-call(bf16[128,72,128]{2,1,0:T(8,128)(2,1)} %all_to_all.20.in_ref), custom_call_target="tpu_custom_call" | custom-call | tf_op jit(solution)/shard_map/pallas_call | solution.py:270
  93.7 27.8 %all_to_all.21.t_ref = bf16[128,36,128]{2,1,0:T(8,128)(2,1)} all-to-all(bf16[128,36,128]{2,1,0:T(8,128)(2,1)} %shard_map.101), channel_id=1, replica_groups=mesh['row'=8,'col'=16] {'row','col'}, dimensions={0} | all-to-all | bytes 2359296 | tf_op jit(solution)/shard_map/all_to_all | solution.py:315
  121.5 12.2 %shard_map.102 = (bf16[128,72,128]{2,1,0:T(8,128)(2,1)}, f32[128,4608]{1,0:T(8,128)}, bf16[128,4608]{1,0:T(8,128)(2,1)}) custom-call(bf16[128,36,128]{2,1,0:T(8,128)(2,1)} %all_to_all.21.t_ref, bf16[128,4608]{1,0:T(8,128)(2,1)} %get-tuple-element.12.current_in, f32[128,4608]{1,0:T(8,128)} %get-tuple-element.13.gating_in, f32[36,128]{1,0:T(8,128)} %mul.34.mask_ref, ...), custom_call_target="tpu_custom_call" | custom-call | tf_op jit(solution)/shard_map/pallas_call | solution.py:270
  133.7 38.0 %all_to_all.22.in_ref = bf16[128,72,128]{2,1,0:T(8,128)(2,1)} all-to-all(bf16[128,72,128]{2,1,0:T(8,128)(2,1)} %get-tuple-element.14), channel_id=1, replica_groups=mesh['row'=8,'col'=16] {'row','col'}, dimensions={0} | all-to-all | bytes 4718592 | tf_op jit(solution)/shard_map/all_to_all | solution.py:315
  171.7 40.0 %shard_map.103 = bf16[128,36,128]{2,1,0:T(8,128)(2,1)} custom-call(bf16[128,72,128]{2,1,0:T(8,128)(2,1)} %all_to_all.22.in_ref), custom_call_target="tpu_custom_call" | custom-call | tf_op jit(solution)/shard_map/pallas_call | solution.py:270
  211.7 27.8 %all_to_all.23.t_ref = bf16[128,36,128]{2,1,0:T(8,128)(2,1)} all-to-all(bf16[128,36,128]{2,1,0:T(8,128)(2,1)} %shard_map.103), channel_id=1, replica_groups=mesh['row'=8,'col'=16] {'row','col'}, dimensions={0} | all-to-all | bytes 2359296 | tf_op jit(solution)/shard_map/all_to_all | solution.py:315
  239.5 11.6 %shard_map.104 = bf16[96,48,128]{2,1,0:T(8,128)(2,1)} custom-call(bf16[128,36,128]{2,1,0:T(8,128)(2,1)} %all_to_all.23.t_ref, bf16[128,4608]{1,0:T(8,128)(2,1)} %get-tuple-element.15.current_in, f32[128,4608]{1,0:T(8,128)} %get-tuple-element.16.gating_in, bf16[128,128]{1,0:T(8,128)(2,1)} %z_ref.3, bf16[128,512]{1,0:T(8,128)(2,1)} %up_ref.1, ...), custom_call_target="tpu_custom_call" | custom-call | tf_op jit(solution)/shard_map/pallas_call | solution.py:270

commit v3 on v2

--- a/solution.py
+++ b/solution.py
@@ -12,7 +12,8 @@
 LANES = 128
 SUB = 8
 RUN = 16
-GROUP = 4
+GROUP = 12
+AT_ONCE = 12
 BF16 = jnp.bfloat16
 F32 = jnp.float32
 
@@ -56,7 +57,7 @@
         out_ref[i] = flat[pl.ds(pl.multiple_of(i * rows, 4), rows), :].astype(out_ref.dtype)
         return 0
 
-    lax.fori_loop(0, n, step, 0, unroll=4)
+    lax.fori_loop(0, n, step, 0, unroll=8)
 
 
 def unpack(in_ref, flat):
@@ -66,7 +67,7 @@
         flat[pl.ds(pl.multiple_of(i * rows, 4), rows), :] = in_ref[i].astype(F32)
         return 0
 
-    lax.fori_loop(0, n, step, 0, unroll=4)
+    lax.fori_loop(0, n, step, 0, unroll=8)
 
 
 def group_mask(mask_ref, chunk):
@@ -178,89 +179,110 @@
 
 def triangle_kernel(n_row, n_col, n_a, n_b, outgoing, in_ref, out_ref, flat, mats, sums, flat_out):
     chunks = n_a * n_b
-    size = n_row * n_a * SUB
     tile = n_row * n_a
+    tiles = 2 * n_b
     unpack(in_ref, flat)
 
-    def place(a, parity, b, a_lo):
+    def place(a, a_lo):
         t = a // (n_a // 2)
         rest = a % (n_a // 2)
         return t * (n_b * LANES) + (rest // 2) * LANES + (rest % 2) * SUB + a_lo
 
+    def enter(operand, scatter, i):
+        column = i // (n_a // AT_ONCE)
+        parity, b = column // n_b, column % n_b
+        first = (i % (n_a // AT_ONCE)) * AT_ONCE
+        for pair in range(AT_ONCE // 2):
+            parts = []
+            for c in range(8):
+                rows = [
+                    flat[
+                        pl.ds(
+                            (2 * c + parity) * 2 * chunks
+                            + operand * chunks + b * n_a + first + 2 * pair + half,
+                            n_row,
+                            stride=n_col * 2 * chunks,
+                        ),
+                        :,
+                    ]
+                    for half in range(2)
+                ]
+                parts.append(jnp.concatenate(rows, axis=0).astype(BF16))
+            parts = exchange(parts)
+            for a_lo in range(8):
+                if scatter:
+                    wide = parts[a_lo].astype(F32)
+                    for half in range(2):
+                        start = place(first + 2 * pair + half, a_lo)
+                        sums[column, pl.ds(start, n_row, stride=RUN), :] = (
+                            wide[half * n_row : (half + 1) * n_row]
+                        )
+                else:
+                    start = a_lo * tile + (first + 2 * pair) * n_row
+                    mats[operand, column, pl.ds(pl.multiple_of(start, 16), 16), :] = (
+                        parts[a_lo]
+                    )
+
+    def loop(n, f):
+        def step(i, _):
+            f(i)
+            return 0
+
+        lax.fori_loop(0, n, step, 0)
+
     for operand in range(2):
         scatter = outgoing and operand == 1
-        for parity in range(2):
-            for b in range(n_b):
-                column = (parity * n_b + b) * LANES
-
-                def step(i, _, operand=operand, scatter=scatter, parity=parity, b=b, column=column):
-                    halves = []
-                    for half in range(2):
-                        a = i * 2 + half
-                        parts = [
-                            flat[
-                                pl.ds(
-                                    (2 * c + parity) * 2 * chunks + operand * chunks + b * n_a + a,
-                                    n_row,
-                                    stride=n_col * 2 * chunks,
-                                ),
-                                :,
-                            ]
-                            for c in range(8)
-                        ]
-                        halves.append(exchange(parts))
-                    for a_lo in range(8):
-                        if scatter:
-                            for half in range(2):
-                                start = place(i * 2 + half, parity, b, a_lo)
-                                sums[column // LANES, pl.ds(start, n_row, stride=RUN), :] = (
-                                    halves[half][a_lo]
-                                )
-                        else:
-                            both = jnp.concatenate([halves[0][a_lo], halves[1][a_lo]], axis=0)
-                            mats[
-                                operand,
-                                pl.ds(pl.multiple_of(a_lo * tile + i * 16, 16), 16),
-                                column : column + LANES,
-                            ] = both.astype(BF16)
-                    return 0
-
-                lax.fori_loop(0, n_a // 2, step, 0)
+        loop(tiles * n_a // AT_ONCE, functools.partial(enter, operand, scatter))
         if scatter:
-            for n in range(size // LANES):
-                mats[operand, :, n * LANES : (n + 1) * LANES] = sums[n].astype(BF16)
-    width = 2 * LANES
-    for n in range(size // width):
-        here = slice(n * width, (n + 1) * width)
+            for n in range(tiles):
+                mats[operand, n] = sums[n].astype(BF16)
+
+    whole = jnp.concatenate([mats[0, n] for n in range(tiles)], axis=1)
+    for n in range(tiles // 2):
         if outgoing:
-            form, right = (((1,), (1,)), ((), ())), mats[1, here, :]
+            rows = slice(2 * n * LANES, (2 * n + 2) * LANES)
+            right = jnp.concatenate([mats[1, k, rows] for k in range(tiles)], axis=1)
+            form = (((1,), (1,)), ((), ()))
         else:
-            form, right = (((0,), (0,)), ((), ())), mats[1, :, here]
-        total = lax.dot_general(mats[0], right, form, preferred_element_type=F32)
+            right = jnp.concatenate([mats[1, 2 * n], mats[1, 2 * n + 1]], axis=1)
+            form = (((0,), (0,)), ((), ()))
+        total = lax.dot_general(whole, right, form, preferred_element_type=F32)
         for j in range(2):
             sums[2 * n + j] = total[:, j * LANES : (j + 1) * LANES]
-    for parity in range(2):
-        for b in range(n_b):
-            column = (parity * n_b + b) * LANES
-
-            def leave(a, _, parity=parity, b=b, column=column):
-                parts = []
-                for a_lo in range(8):
-                    if outgoing:
-                        rows = pl.ds(pl.multiple_of(a_lo * tile + a * 8, 8), n_row)
-                    else:
-                        rows = pl.ds(place(a, parity, b, a_lo), n_row, stride=RUN)
-                    parts.append(sums[column // LANES, rows, :])
-                for c, part in enumerate(exchange(parts)):
+
+    def leave(i):
+        column = i // (n_a // AT_ONCE)
+        parity, b = column // n_b, column % n_b
+        first = (i % (n_a // AT_ONCE)) * AT_ONCE
+        for pair in range(AT_ONCE // 2):
+            a = first + 2 * pair
+            parts = []
+            for a_lo in range(8):
+                if outgoing:
+                    start = a_lo * tile + a * n_row
+                    value = sums[column, pl.ds(pl.multiple_of(start, 16), 16), :]
+                else:
+                    value = jnp.concatenate(
+                        [
+                            sums[column, pl.ds(place(a + half, a_lo), n_row, stride=RUN), :]
+                            for half in range(2)
+                        ],
+                        axis=0,
+                    )
+                parts.append(value.astype(BF16))
+            for c, part in enumerate(exchange(parts)):
+                wide = part.astype(F32)
+                for half in range(2):
                     flat_out[
                         pl.ds(
-                            (2 * c + parity) * chunks + b * n_a + a, n_row, stride=n_col * chunks
+                            (2 * c + parity) * chunks + b * n_a + a + half,
+                            n_row,
+                            stride=n_col * chunks,
                         ),
                         :,
-                    ] = part
-                return 0
-
-            lax.fori_loop(0, n_a, leave, 0)
+                    ] = wide[half * n_row : (half + 1) * n_row]
+
+    loop(tiles * n_a // AT_ONCE, leave)
     pack(flat_out, out_ref)
 
 
@@ -319,7 +341,7 @@
             call(
                 functools.partial(triangle_kernel, n_row, n_col, n_a, n_b, outgoing),
                 shape((n_row * n_col, chunks, LANES), BF16),
-                [flat_two, pltpu.VMEM((2, size, size), BF16), pltpu.VMEM((size // LANES, size, LANES), F32), flat_one],
+                [flat_two, pltpu.VMEM((2, size // LANES, size, LANES), BF16), pltpu.VMEM((size // LANES, size, LANES), F32), flat_one],
                 move(both),
             )
         )

time: 252 us -> 189 us (0.75)
  Pallas kernels: 111 us -> 49.1 us
    pallas_call x5, Pallas kernels: 111 us -> 49.1 us  [call(): pl.pallas_call(kernel, out_shape=outs, in_specs=[vmem] * len(args), out_s...]
where the time goes in v3:
time: 189 us
  blocking collectives  138 us (73%)
  Pallas kernels  49.1 us (26%)
    all_to_all x4, blocking collectives, move(): return lax.all_to_all(x, AXES, 0, 0, tiled=True)  138 us
    pallas_call x5, Pallas kernels, call(): pl.pallas_call(kernel, out_shape=outs, in_specs=[vmem] * len(args), out_s...  49.1 us

profile of v3, /device:TPU:1, one launch (start us, length us, event | category | flops | bytes accessed | tf_op | source)
XLA Modules:
  0.0 188.8 jit_solution(6440112568961012457)
XLA Ops:
  0.0 0.7 convert_element_type.3
  0.7 0.1 dynamic_slice.7
  0.8 0.1 dynamic_slice.6
  0.8 0.1 mul.31
  0.9 0.1 mul.28
  1.0 0.1 broadcast_multiply_fusion
  1.1 0.7 mul.34.mask_ref
  1.8 7.3 %shard_map.100 = (bf16[128,72,128]{2,1,0:T(8,128)(2,1)}, f32[128,4608]{1,0:T(8,128)}, bf16[128,4608]{1,0:T(8,128)(2,1)}) custom-call(bf16[96,48,128]{2,1,0:T(8,128)(2,1)} %x_ref.1, f32[36,128]{1,0:T(8,128)} %mul.34.mask_ref, bf16[128,512]{1,0:T(8,128)(2,1)} %ab_ref.2, bf16[128,128]{1,0:T(8,128)(2,1)} %gate_ref.2), custom_call_target="tpu_custom_call" | custom-call | tf_op jit(solution)/shard_map/pallas_call | solution.py:292
  9.1 44.3 %all_to_all.20.in_ref = bf16[128,72,128]{2,1,0:T(8,128)(2,1)} all-to-all(bf16[128,72,128]{2,1,0:T(8,128)(2,1)} %get-tuple-element.11), channel_id=1, replica_groups=mesh['row'=8,'col'=16] {'row','col'}, dimensions={0} | all-to-all | bytes 4718592 | tf_op jit(solution)/shard_map/all_to_all | solution.py:337
  53.4 12.3 %shard_map.101 = bf16[128,36,128]{2,1,0:T(8,128)(2,1)} custom-call(bf16[128,72,128]{2,1,0:T(8,128)(2,1)} %all_to_all.20.in_ref), custom_call_target="tpu_custom_call" | custom-call | tf_op jit(solution)/shard_map/pallas_call | solution.py:292
  65.7 27.8 %all_to_all.21.t_ref = bf16[128,36,128]{2,1,0:T(8,128)(2,1)} all-to-all(bf16[128,36,128]{2,1,0:T(8,128)(2,1)} %shard_map.101), channel_id=1, replica_groups=mesh['row'=8,'col'=16] {'row','col'}, dimensions={0} | all-to-all | bytes 2359296 | tf_op jit(solution)/shard_map/all_to_all | solution.py:337
  93.4 9.6 %shard_map.102 = (bf16[128,72,128]{2,1,0:T(8,128)(2,1)}, f32[128,4608]{1,0:T(8,128)}, bf16[128,4608]{1,0:T(8,128)(2,1)}) custom-call(bf16[128,36,128]{2,1,0:T(8,128)(2,1)} %all_to_all.21.t_ref, bf16[128,4608]{1,0:T(8,128)(2,1)} %get-tuple-element.12.current_in, f32[128,4608]{1,0:T(8,128)} %get-tuple-element.13.gating_in, f32[36,128]{1,0:T(8,128)} %mul.34.mask_ref, ...), custom_call_target="tpu_custom_call" | custom-call | tf_op jit(solution)/shard_map/pallas_call | solution.py:292
  103.0 38.0 %all_to_all.22.in_ref = bf16[128,72,128]{2,1,0:T(8,128)(2,1)} all-to-all(bf16[128,72,128]{2,1,0:T(8,128)(2,1)} %get-tuple-element.14), channel_id=1, replica_groups=mesh['row'=8,'col'=16] {'row','col'}, dimensions={0} | all-to-all | bytes 4718592 | tf_op jit(solution)/shard_map/all_to_all | solution.py:337
  141.0 12.3 %shard_map.103 = bf16[128,36,128]{2,1,0:T(8,128)(2,1)} custom-call(bf16[128,72,128]{2,1,0:T(8,128)(2,1)} %all_to_all.22.in_ref), custom_call_target="tpu_custom_call" | custom-call | tf_op jit(solution)/shard_map/pallas_call | solution.py:292
  153.3 27.8 %all_to_all.23.t_ref = bf16[128,36,128]{2,1,0:T(8,128)(2,1)} all-to-all(bf16[128,36,128]{2,1,0:T(8,128)(2,1)} %shard_map.103), channel_id=1, replica_groups=mesh['row'=8,'col'=16] {'row','col'}, dimensions={0} | all-to-all | bytes 2359296 | tf_op jit(solution)/shard_map/all_to_all | solution.py:337
  181.1 7.7 %shard_map.104 = bf16[96,48,128]{2,1,0:T(8,128)(2,1)} custom-call(bf16[128,36,128]{2,1,0:T(8,128)(2,1)} %all_to_all.23.t_ref, bf16[128,4608]{1,0:T(8,128)(2,1)} %get-tuple-element.15.current_in, f32[128,4608]{1,0:T(8,128)} %get-tuple-element.16.gating_in, bf16[128,128]{1,0:T(8,128)(2,1)} %z_ref.3, bf16[128,512]{1,0:T(8,128)(2,1)} %up_ref.1, ...), custom_call_target="tpu_custom_call" | custom-call | tf_op jit(solution)/shard_map/pallas_call | solution.py:292

commit v4 on v1

v4 whole, which is shorter than its diff:
```python
import functools

import jax
import jax.numpy as jnp
from jax import lax
from jax.experimental import pallas as pl
from jax.experimental.pallas import tpu as pltpu
from jax.sharding import PartitionSpec as P

EPS = 1e-05
LANES = 128
SUB = 8
RUN = 16
BF16 = jnp.bfloat16
F32 = jnp.float32

SIZES = (4, 4, 8)
ORDERS = ((2, 1, 0), (1, 0, 2), (0, 2, 1))
MESH = pl.DeviceIdType.MESH


def norm(x):
    center = x - jnp.mean(x, axis=0, keepdims=True)
    return center * lax.rsqrt(jnp.mean(center * center, axis=0, keepdims=True) + EPS)


def sigmoid(x):
    return 0.5 * jnp.tanh(0.5 * x) + 0.5


def dot(a, b):
    return jnp.dot(a, b, preferred_element_type=F32)


def turned(w_ref):
    return w_ref[...].astype(F32).T.astype(BF16)


def exchange(parts):
    group = lax.broadcasted_iota(jnp.int32, parts[0].shape, 1) // RUN
    parts = list(parts)
    for bit in (1, 2, 4):
        chosen = (group // bit) % 2 == 1
        for i in range(8):
            if i & bit:
                continue
            low, high = parts[i], parts[i + bit]
            parts[i] = jnp.where(chosen, pltpu.roll(high, RUN * bit, 1), low)
            parts[i + bit] = jnp.where(chosen, high, pltpu.roll(low, LANES - RUN * bit, 1))
    return parts


def coordinates():
    row, col = lax.axis_index("row"), lax.axis_index("col")
    return row // 2, (row % 2) * 2 + (col // 2) % 2, (col // 4) * 2 + col % 2


def device(place):
    z, y, x = place
    return z * 2 + y // 2, (x // 2) * 4 + (y % 2) * 2 + x % 2


def loop(n, f, unroll=1):
    def step(i, _):
        f(i)
        return 0

    lax.fori_loop(0, n, step, 0, unroll=unroll)


def along(ref, axis, at):
    return ref.at[(slice(None),) * axis + (at,)]


class Move:
    def __init__(self, me, buffers, index, send, receive, local):
        self.me, self.buffers, self.index = me, buffers, index
        self.send, self.receive, self.local = send, receive, local

    def parts(self, third, stage):
        axis = ORDERS[third][stage]
        source, target = self.buffers[stage].at[third], self.buffers[stage + 1].at[third]
        return axis, source, target, (self.index, third, stage)

    def start(self, third, stage):
        axis, source, target, at = self.parts(third, stage)
        here = self.me[axis]
        for step in range(1, SIZES[axis]):
            there = (here + step) % SIZES[axis]
            place = list(self.me)
            place[axis] = there
            pltpu.make_async_remote_copy(
                src_ref=along(source, axis, there),
                dst_ref=along(target, axis, here),
                send_sem=self.send.at[at],
                recv_sem=self.receive.at[at],
                device_id=device(place),
                device_id_type=MESH,
            ).start()
        pltpu.make_async_copy(
            along(source, axis, here), along(target, axis, here), self.local.at[at]
        ).start()

    def arrive(self, third, stage):
        axis, source, target, at = self.parts(third, stage)
        most = along(target, axis, slice(1, SIZES[axis]))
        pltpu.make_async_copy(most, most, self.receive.at[at]).wait()
        one = along(target, axis, self.me[axis])
        pltpu.make_async_copy(one, one, self.local.at[at]).wait()

    def sent(self):
        for third in range(3):
            for stage in range(3):
                axis, source, target, at = self.parts(third, stage)
                most = along(source, axis, slice(1, SIZES[axis]))
                pltpu.make_async_copy(most, most, self.send.at[at]).wait()

    def advance(self):
        for stage in (1, 2):
            for third in range(3):
                self.arrive(third, stage - 1)
                self.start(third, stage)

    def at_third(self, third, act):
        for one in range(3):
            pl.when(third == one)(functools.partial(act, one))

    def begin(self, third):
        self.at_third(third, lambda one: self.start(one, 0))

    def end(self, third):
        self.at_third(third, lambda one: self.arrive(one, 2))


def put(flat, buffer, third, by_device):
    rows = buffer.shape[4]

    def one(i):
        place = (i // 32, (i // 8) % 4, i % 8)
        first = i
        if by_device:
            row, col = device(place)
            first = row * 16 + col
        buffer[(third,) + place] = flat[pl.ds(pl.multiple_of(first * rows, 4), rows), :].astype(
            BF16
        )

    loop(128, one, 8)


def take(buffer, flat, third, by_device):
    rows = buffer.shape[4]

    def one(i):
        place = (i // 32, (i // 8) % 4, i % 8)
        first = i
        if by_device:
            row, col = device(place)
            first = row * 16 + col
        flat[pl.ds(pl.multiple_of(first * rows, 4), rows), :] = buffer[(third,) + place].astype(F32)

    loop(128, one, 8)


def kernel(
    x_ref, mask_ref, ab1_ref, gate1_ref, z1_ref, ab2_ref, gate2_ref, z2_ref, up_ref, down_ref,
    out_ref,
    current_ref, gating_ref, flat_two, flat_one, mats, sums,
    p0, p1, p2, p3, q0, q1, q2, q3, r0, r1, r2, r3, s0, s1, s2, s3,
    send, receive, local,
):
    n_row, n_col = 8, 16
    rows, cols, channels = x_ref.shape
    n_a, n_b = rows // SUB, cols // RUN
    width = n_a * LANES
    tile = n_row * n_a
    tiles = 2 * n_b
    me = coordinates()
    moves = [
        Move(me, buffers, index, send, receive, local)
        for index, buffers in enumerate(
            ((p0, p1, p2, p3), (q0, q1, q2, q3), (r0, r1, r2, r3), (s0, s1, s2, s3))
        )
    ]

    barrier = pltpu.get_barrier_semaphore()
    for axis in range(3):
        for step in range(1, SIZES[axis]):
            place = list(me)
            place[axis] = (me[axis] + step) % SIZES[axis]
            pl.semaphore_signal(barrier, inc=1, device_id=device(place), device_id_type=MESH)

    def lanes_of(third):
        return pl.ds(pl.multiple_of(third * width, LANES), width)

    def emit(third, current, ab, gate, move):
        normed = norm(current).astype(BF16)
        hidden = ab.shape[0] // 4
        mask = jnp.concatenate([mask_ref[pl.ds(third * n_a + j, 1), :] for j in range(n_a)], axis=1)
        p = dot(ab, normed)
        left = mask * sigmoid(p[hidden : 2 * hidden]) * p[:hidden]
        right = mask * sigmoid(p[3 * hidden :]) * p[2 * hidden : 3 * hidden]
        for j in range(n_a):
            lanes = slice(j * LANES, (j + 1) * LANES)
            flat_two[pl.ds(j, hidden, stride=2 * n_a), :] = left[:, lanes]
            flat_two[pl.ds(n_a + j, hidden, stride=2 * n_a), :] = right[:, lanes]
        gating_ref[:, lanes_of(third)] = sigmoid(dot(gate, normed))
        put(flat_two, move.buffers[0], third, False)

    def finish(third, z, move):
        take(move.buffers[3], flat_one, third, False)
        triangle = jnp.concatenate(
            [flat_one[pl.ds(j, channels, stride=n_a), :] for j in range(n_a)], axis=1
        )
        here = lanes_of(third)
        update = gating_ref[:, here] * dot(z, norm(triangle).astype(BF16))
        return (current_ref[:, here].astype(F32) + update).astype(BF16)

    def place_of(a, a_lo):
        t = a // (n_a // 2)
        rest = a % (n_a // 2)
        return t * (n_b * LANES) + (rest // 2) * LANES + (rest % 2) * SUB + a_lo

    def triangle(outgoing, inward, outward):
        def enter(third):
            inward.end(third)
            take(inward.buffers[3], flat_two, third, True)
            for operand in range(2):
                scatter = outgoing and operand == 1

                def one(parity, operand=operand, scatter=scatter):
                    column = parity * n_b + third
                    for a in range(0, n_a, 2):
                        parts = []
                        for c in range(8):
                            pieces = [
                                flat_two[
                                    pl.ds(
                                        (2 * c + parity) * 2 * n_a + operand * n_a + a + half,
                                        n_row,
                                        stride=n_col * 2 * n_a,
                                    ),
                                    :,
                                ]
                                for half in range(2)
                            ]
                            parts.append(jnp.concatenate(pieces, axis=0).astype(BF16))
                        parts = exchange(parts)
                        for a_lo in range(8):
                            if scatter:
                                wide = parts[a_lo].astype(F32)
                                for half in range(2):
                                    start = place_of(a + half, a_lo)
                                    sums[column, pl.ds(start, n_row, stride=RUN), :] = (
                                        wide[half * n_row : (half + 1) * n_row]
                                    )
                            else:
                                start = a_lo * tile + a * n_row
                                mats[operand, column, pl.ds(start, 16), :] = parts[a_lo]
                    if scatter:
                        mats[operand, column] = sums[column].astype(BF16)

                loop(2, one)

        loop(n_b, enter)
        whole = jnp.concatenate([mats[0, n] for n in range(tiles)], axis=1)
        for n in range(tiles // 2):
            if outgoing:
                here = slice(2 * n * LANES, (2 * n + 2) * LANES)
                right = jnp.concatenate([mats[1, k, here] for k in range(tiles)], axis=1)
                form = (((1,), (1,)), ((), ()))
            else:
                right = jnp.concatenate([mats[1, 2 * n], mats[1, 2 * n + 1]], axis=1)
                form = (((0,), (0,)), ((), ()))
            total = lax.dot_general(whole, right, form, preferred_element_type=F32)
            for j in range(2):
                sums[2 * n + j] = total[:, j * LANES : (j + 1) * LANES]

        def leave(third):
            def one(parity):
                column = parity * n_b + third
                for a in range(0, n_a, 2):
                    parts = []
                    for a_lo in range(8):
                        if outgoing:
                            value = sums[column, pl.ds(a_lo * tile + a * n_row, 16), :]
                        else:
                            value = jnp.concatenate(
                                [
                                    sums[column, pl.ds(place_of(a + half, a_lo), n_row, stride=RUN), :]
                                    for half in range(2)
                                ],
                                axis=0,
                            )
                        parts.append(value.astype(BF16))
                    for c, part in enumerate(exchange(parts)):
                        wide = part.astype(F32)
                        for half in range(2):
                            flat_one[
                                pl.ds(
                                    (2 * c + parity) * n_a + a + half, n_row, stride=n_col * n_a
                                ),
                                :,
                            ] = wide[half * n_row : (half + 1) * n_row]

            loop(2, one)
            put(flat_one, outward.buffers[0], third, True)
            outward.begin(third)

        loop(n_b, leave)

    ab, gate = turned(ab1_ref), turned(gate1_ref)

    def first(third):
        block = x_ref[:, pl.ds(pl.multiple_of(third * RUN, RUN), RUN), :]
        current = block.astype(F32).reshape(width, channels).T
        current_ref[:, lanes_of(third)] = current.astype(BF16)
        emit(third, current, ab, gate, moves[0])
        pl.when(third == 0)(lambda: pl.semaphore_wait(barrier, sum(SIZES) - 3))
        moves[0].begin(third)

    loop(n_b, first)
    moves[0].advance()
    triangle(True, moves[0], moves[1])

    z, ab2, gate2 = turned(z1_ref), turned(ab2_ref), turned(gate2_ref)
    moves[1].advance()

    def middle(third):
        moves[1].end(third)
        current = finish(third, z, moves[1])
        current_ref[:, lanes_of(third)] = current
        emit(third, current.astype(F32), ab2, gate2, moves[2])
        moves[2].begin(third)

    loop(n_b, middle)
    moves[2].advance()
    triangle(False, moves[2], moves[3])

    z2, up, down = turned(z2_ref), turned(up_ref), turned(down_ref)
    moves[3].advance()

    def last(third):
        moves[3].end(third)
        current = finish(third, z2, moves[3]).astype(F32)
        expanded = jnp.maximum(dot(up, norm(current).astype(BF16)), 0.0).astype(BF16)
        result = current + dot(down, expanded)
        out_ref[:, pl.ds(pl.multiple_of(third * RUN, RUN), RUN), :] = result.T.reshape(
            rows, RUN, channels
        ).astype(out_ref.dtype)

    loop(n_b, last)
    for move in moves:
        move.sent()


def body(
    pair,
    residue_mask,
    out_ab_weight,
    out_gate_weight,
    out_z_weight,
    in_ab_weight,
    in_gate_weight,
    in_z_weight,
    trans_up,
    trans_down,
):
    rows, cols, channels = pair.shape
    n_a, n_b = rows // SUB, cols // RUN
    chunks = n_a * n_b
    size = 8 * rows
    present = residue_mask.astype(F32)
    mask_rows = lax.dynamic_slice_in_dim(present, lax.axis_index("row") * rows, rows)
    mask_cols = lax.dynamic_slice_in_dim(present, lax.axis_index("col") * cols, cols)
    mask = (
        mask_rows.reshape(1, n_a, SUB, 1) * mask_cols.reshape(n_b, 1, 1, RUN)
    ).reshape(chunks, LANES)
    vmem = pl.BlockSpec(memory_space=pltpu.VMEM)
    two = pltpu.VMEM((n_b,) + SIZES + (2 * n_a, LANES), BF16)
    one = pltpu.VMEM((n_b,) + SIZES + (n_a, LANES), BF16)
    return pl.pallas_call(
        kernel,
        out_shape=jax.ShapeDtypeStruct(pair.shape, pair.dtype),
        in_specs=[vmem] * 10,
        out_specs=vmem,
        scratch_shapes=[
            pltpu.VMEM((channels, chunks * LANES), BF16),
            pltpu.VMEM((channels, chunks * LANES), F32),
            pltpu.VMEM((128 * 2 * n_a, LANES), F32),
            pltpu.VMEM((128 * n_a, LANES), F32),
            pltpu.VMEM((2, size // LANES, size, LANES), BF16),
            pltpu.VMEM((size // LANES, size, LANES), F32),
            *([two] * 4 + [one] * 4) * 2,
            pltpu.SemaphoreType.DMA((4, 3, 3)),
            pltpu.SemaphoreType.DMA((4, 3, 3)),
            pltpu.SemaphoreType.DMA((4, 3, 3)),
        ],
        compiler_params=pltpu.CompilerParams(
            collective_id=0, has_side_effects=True, vmem_limit_bytes=60 << 20
        ),
    )(
        pair, mask, out_ab_weight, out_gate_weight, out_z_weight, in_ab_weight, in_gate_weight,
        in_z_weight, trans_up, trans_down,
    )


def solution(mesh):
    placed = (P("row", "col", None), P(), P(), P(), P(), P(), P(), P(), P(), P())
    return jax.shard_map(
        body, mesh=mesh, in_specs=placed, out_specs=P("row", "col", None), check_vma=False
    )
```

time: 341 us -> 194 us (0.57); the launches traced: 334 us -> 193 us
  Pallas kernels: 0 us -> 189 us
  local copies, waits for them, and re-layouts: 129 us -> 3.38 us
  blocking collectives: 82.4 us -> 0 us
  other arithmetic: 50.7 us -> 0.78 us
  waiting for transfers between devices: 34.1 us -> 0 us
  matrix products: 24.7 us -> 0 us
  starting transfers between devices: 12 us -> 0 us
    pallas_call x0 -> x1, Pallas kernels: none -> 189 us  [body(): pl.pallas_call(kernel, out_shape=jax.ShapeDtypeStruct(pair.shape, pair.dt...]
    all_to_all x2 -> x0, blocking collectives: 82.4 us -> none  [triangle(): moved = lax.all_to_all(both, AXES, 0, 0, tiled=True)]
    all_to_all x2 -> x0, waiting for transfers between devices: 34.1 us -> none  [triangle(): lax.all_to_all(sums.reshape(hidden, rows * cols), AXES, 0, 0, tiled=True)]
    slice x6 -> x0, local copies, waits for them, and re-layouts: 28.6 us -> none  [the longest x4 19.8 us: triangle(): whole[1]]
    dot_general x9 -> x0, matrix products: 24.7 us -> none  [the longest x7 18.6 us: project(): lax.dot_general(weight, normed, (((0,), (0,)), ((), ())), preferred_eleme...]
    reshape x4 -> x0, local copies, waits for them, and re-layouts: 23.6 us -> none  [the longest x2 17 us: triangle(): whole = moved.reshape(n_row, n_col, 2, rows, cols).transpose(2, 0, 3, 1, 4)]
    all_to_all x5 -> x0, local copies, waits for them, and re-layouts: 18.8 us -> none  [the longest x3 16.9 us: triangle(): lax.all_to_all(sums.reshape(hidden, rows * cols), AXES, 0, 0, tiled=True)]
    all_to_all x2 -> x0, other arithmetic: 18.6 us -> none  [triangle(): lax.all_to_all(sums.reshape(hidden, rows * cols), AXES, 0, 0, tiled=True)]
  transfers between devices with their start and end apart: 2 -> 0, of which waited for: 2 -> 0; matrix products, arithmetic and copies ran while one was open for 2% -> 0% of each run, Pallas kernels for 0% -> 0%
where the time goes in v4:
time: 194 us; the launch traced here: 193 us
  Pallas kernels  189 us (97%)
  local copies, waits for them, and re-layouts  3.38 us (2%)
    pallas_call x1, Pallas kernels, body(): pl.pallas_call(kernel, out_shape=jax.ShapeDtypeStruct(pair.shape, pair.dt...  189 us

profile of v4, /device:TPU:1, one launch (start us, length us, event | category | flops | bytes accessed | tf_op | source)
XLA Modules:
  0.0 193.0 jit_solution(14917307071261638803)
XLA Ops:
  0.0 0.7 convert_element_type.3
  0.7 0.1 dynamic_slice.7
  0.8 0.1 dynamic_slice.6
  0.8 0.1 mul.31
  0.9 0.1 mul.28
  1.0 0.1 broadcast_multiply_fusion
  1.1 0.7 mul.34.mask_ref
  1.8 188.9 %shard_map.100 = bf16[96,48,128]{2,1,0:T(8,128)(2,1)} custom-call(bf16[96,48,128]{2,1,0:T(8,128)(2,1)} %x_ref.1, f32[36,128]{1,0:T(8,128)} %mul.34.mask_ref, bf16[128,512]{1,0:T(8,128)(2,1)} %ab1_ref.1, bf16[128,128]{1,0:T(8,128)(2,1)} %gate1_ref.1, bf16[128,128]{1,0:T(8,128)(2,1)} %z1_ref.1, bf16[128,512]{1,0:T(8,128)(2,1)} %ab2_ref.1, ...), custom_call_target="tpu_custom_call" | custom-call | tf_op jit(solution)/shard_map/pallas_call | solution.py:382
  190.7 2.4 %copy.12 = bf16[96,48,128]{2,1,0:T(8,128)(2,1)} copy(bf16[96,48,128]{2,1,0:T(8,128)(2,1)} %shard_map.100) | data formatting | bytes 2359296

commit v5 on v4

--- a/solution.py
+++ b/solution.py
@@ -14,8 +14,9 @@
 BF16 = jnp.bfloat16
 F32 = jnp.float32
 
-SIZES = (4, 4, 8)
-ORDERS = ((2, 1, 0), (1, 0, 2), (0, 2, 1))
+SIZES = (16, 8)
+ORDERS = ((1, 0), (0, 1), (1, 0))
+STAGES = 2
 MESH = pl.DeviceIdType.MESH
 
 
@@ -52,12 +53,12 @@
 
 def coordinates():
     row, col = lax.axis_index("row"), lax.axis_index("col")
-    return row // 2, (row % 2) * 2 + (col // 2) % 2, (col // 4) * 2 + col % 2
+    return row * 2 + (col // 2) % 2, (col // 4) * 2 + col % 2
 
 
 def device(place):
-    z, y, x = place
-    return z * 2 + y // 2, (x // 2) * 4 + (y % 2) * 2 + x % 2
+    plane, x = place
+    return plane // 2, (x // 2) * 4 + (plane % 2) * 2 + x % 2
 
 
 def loop(n, f, unroll=1):
@@ -110,13 +111,13 @@
 
     def sent(self):
         for third in range(3):
-            for stage in range(3):
+            for stage in range(STAGES):
                 axis, source, target, at = self.parts(third, stage)
                 most = along(source, axis, slice(1, SIZES[axis]))
                 pltpu.make_async_copy(most, most, self.send.at[at]).wait()
 
     def advance(self):
-        for stage in (1, 2):
+        for stage in range(1, STAGES):
             for third in range(3):
                 self.arrive(third, stage - 1)
                 self.start(third, stage)
@@ -129,44 +130,37 @@
         self.at_third(third, lambda one: self.start(one, 0))
 
     def end(self, third):
-        self.at_third(third, lambda one: self.arrive(one, 2))
-
-
-def put(flat, buffer, third, by_device):
-    rows = buffer.shape[4]
-
-    def one(i):
-        place = (i // 32, (i // 8) % 4, i % 8)
-        first = i
-        if by_device:
-            row, col = device(place)
-            first = row * 16 + col
-        buffer[(third,) + place] = flat[pl.ds(pl.multiple_of(first * rows, 4), rows), :].astype(
-            BF16
+        self.at_third(third, lambda one: self.arrive(one, STAGES - 1))
+
+
+def put(flat, buffer, third):
+    planes, places, rows = buffer.shape[1:4]
+
+    def one(plane):
+        block = flat[pl.ds(pl.multiple_of(plane * places * rows, 8), places * rows), :]
+        for x in range(places):
+            buffer[third, plane, x] = block[x * rows : (x + 1) * rows].astype(BF16)
+
+    loop(planes, one, 2)
+
+
+def take(buffer, flat, third):
+    planes, places, rows = buffer.shape[1:4]
+
+    def one(plane):
+        block = [buffer[third, plane, x].astype(F32) for x in range(places)]
+        flat[pl.ds(pl.multiple_of(plane * places * rows, 8), places * rows), :] = jnp.concatenate(
+            block, axis=0
         )
 
-    loop(128, one, 8)
-
-
-def take(buffer, flat, third, by_device):
-    rows = buffer.shape[4]
-
-    def one(i):
-        place = (i // 32, (i // 8) % 4, i % 8)
-        first = i
-        if by_device:
-            row, col = device(place)
-            first = row * 16 + col
-        flat[pl.ds(pl.multiple_of(first * rows, 4), rows), :] = buffer[(third,) + place].astype(F32)
-
-    loop(128, one, 8)
+    loop(planes, one, 2)
 
 
 def kernel(
     x_ref, mask_ref, ab1_ref, gate1_ref, z1_ref, ab2_ref, gate2_ref, z2_ref, up_ref, down_ref,
     out_ref,
     current_ref, gating_ref, flat_two, flat_one, mats, sums,
-    p0, p1, p2, p3, q0, q1, q2, q3, r0, r1, r2, r3, s0, s1, s2, s3,
+    p0, p1, p2, q0, q1, q2, r0, r1, r2, s0, s1, s2,
     send, receive, local,
 ):
     n_row, n_col = 8, 16
@@ -179,12 +173,12 @@
     moves = [
         Move(me, buffers, index, send, receive, local)
         for index, buffers in enumerate(
-            ((p0, p1, p2, p3), (q0, q1, q2, q3), (r0, r1, r2, r3), (s0, s1, s2, s3))
+            ((p0, p1, p2), (q0, q1, q2), (r0, r1, r2), (s0, s1, s2))
         )
     ]
 
     barrier = pltpu.get_barrier_semaphore()
-    for axis in range(3):
+    for axis in range(len(SIZES)):
         for step in range(1, SIZES[axis]):
             place = list(me)
             place[axis] = (me[axis] + step) % SIZES[axis]
@@ -205,10 +199,10 @@
             flat_two[pl.ds(j, hidden, stride=2 * n_a), :] = left[:, lanes]
             flat_two[pl.ds(n_a + j, hidden, stride=2 * n_a), :] = right[:, lanes]
         gating_ref[:, lanes_of(third)] = sigmoid(dot(gate, normed))
-        put(flat_two, move.buffers[0], third, False)
+        put(flat_two, move.buffers[0], third)
 
     def finish(third, z, move):
-        take(move.buffers[3], flat_one, third, False)
+        take(move.buffers[STAGES], flat_one, third)
         triangle = jnp.concatenate(
             [flat_one[pl.ds(j, channels, stride=n_a), :] for j in range(n_a)], axis=1
         )
@@ -221,10 +215,13 @@
         rest = a % (n_a // 2)
         return t * (n_b * LANES) + (rest // 2) * LANES + (rest % 2) * SUB + a_lo
 
+    def place_at(c):
+        return (c % 2) * 8 + (c // 2) * 2
+
     def triangle(outgoing, inward, outward):
         def enter(third):
             inward.end(third)
-            take(inward.buffers[3], flat_two, third, True)
+            take(inward.buffers[STAGES], flat_two, third)
             for operand in range(2):
                 scatter = outgoing and operand == 1
 
@@ -236,7 +233,7 @@
                             pieces = [
                                 flat_two[
                                     pl.ds(
-                                        (2 * c + parity) * 2 * n_a + operand * n_a + a + half,
+                                        (place_at(c) + parity) * 2 * n_a + operand * n_a + a + half,
                                         n_row,
                                         stride=n_col * 2 * n_a,
                                     ),
@@ -298,13 +295,15 @@
                         for half in range(2):
                             flat_one[
                                 pl.ds(
-                                    (2 * c + parity) * n_a + a + half, n_row, stride=n_col * n_a
+                                    (place_at(c) + parity) * n_a + a + half,
+                                    n_row,
+                                    stride=n_col * n_a,
                                 ),
                                 :,
                             ] = wide[half * n_row : (half + 1) * n_row]
 
             loop(2, one)
-            put(flat_one, outward.buffers[0], third, True)
+            put(flat_one, outward.buffers[0], third)
             outward.begin(third)
 
         loop(n_b, leave)
@@ -316,7 +315,7 @@
         current = block.astype(F32).reshape(width, channels).T
         current_ref[:, lanes_of(third)] = current.astype(BF16)
         emit(third, current, ab, gate, moves[0])
-        pl.when(third == 0)(lambda: pl.semaphore_wait(barrier, sum(SIZES) - 3))
+        pl.when(third == 0)(lambda: pl.semaphore_wait(barrier, sum(SIZES) - len(SIZES)))
         moves[0].begin(third)
 
     loop(n_b, first)
@@ -391,10 +390,10 @@
             pltpu.VMEM((128 * n_a, LANES), F32),
             pltpu.VMEM((2, size // LANES, size, LANES), BF16),
             pltpu.VMEM((size // LANES, size, LANES), F32),
-            *([two] * 4 + [one] * 4) * 2,
-            pltpu.SemaphoreType.DMA((4, 3, 3)),
-            pltpu.SemaphoreType.DMA((4, 3, 3)),
-            pltpu.SemaphoreType.DMA((4, 3, 3)),
+            *([two] * (STAGES + 1) + [one] * (STAGES + 1)) * 2,
+            pltpu.SemaphoreType.DMA((4, 3, STAGES)),
+            pltpu.SemaphoreType.DMA((4, 3, STAGES)),
+            pltpu.SemaphoreType.DMA((4, 3, STAGES)),
         ],
         compiler_params=pltpu.CompilerParams(
             collective_id=0, has_side_effects=True, vmem_limit_bytes=60 << 20

time: 194 us -> 131 us (0.68)
  Pallas kernels: 189 us -> 126 us
    pallas_call x1, Pallas kernels: 189 us -> 126 us  [body(): pl.pallas_call(kernel, out_shape=jax.ShapeDtypeStruct(pair.shape, pair.dt...]
where the time goes in v5:
time: 131 us
  Pallas kernels  126 us (96%)
  local copies, waits for them, and re-layouts  3.38 us (3%)
    pallas_call x1, Pallas kernels, body(): pl.pallas_call(kernel, out_shape=jax.ShapeDtypeStruct(pair.shape, pair.dt...  126 us

profile of v5, /device:TPU:1, one launch (start us, length us, event | category | flops | bytes accessed | tf_op | source)
XLA Modules:
  0.0 130.5 jit_solution(10430246342369082392)
XLA Ops:
  0.0 0.7 convert_element_type.3
  0.7 0.1 dynamic_slice.7
  0.8 0.1 dynamic_slice.6
  0.8 0.1 mul.31
  0.9 0.1 mul.28
  1.0 0.1 broadcast_multiply_fusion
  1.1 0.7 mul.34.mask_ref
  1.8 126.4 %shard_map.100 = bf16[96,48,128]{2,1,0:T(8,128)(2,1)} custom-call(bf16[96,48,128]{2,1,0:T(8,128)(2,1)} %x_ref.1, f32[36,128]{1,0:T(8,128)} %mul.34.mask_ref, bf16[128,512]{1,0:T(8,128)(2,1)} %ab1_ref.1, bf16[128,128]{1,0:T(8,128)(2,1)} %gate1_ref.1, bf16[128,128]{1,0:T(8,128)(2,1)} %z1_ref.1, bf16[128,512]{1,0:T(8,128)(2,1)} %ab2_ref.1, ...), custom_call_target="tpu_custom_call" | custom-call | tf_op jit(solution)/shard_map/pallas_call | solution.py:381
  128.2 2.4 %copy.12 = bf16[96,48,128]{2,1,0:T(8,128)(2,1)} copy(bf16[96,48,128]{2,1,0:T(8,128)(2,1)} %shard_map.100) | data formatting | bytes 2359296

commit v6 on v5

v6 whole, which is shorter than its diff:
```python
import functools

import jax
import jax.numpy as jnp
from jax import lax
from jax.experimental import pallas as pl
from jax.experimental.pallas import tpu as pltpu
from jax.sharding import PartitionSpec as P

EPS = 1e-05
LANES = 128
SUB = 8
RUN = 16
BF16 = jnp.bfloat16
F32 = jnp.float32

SIZES = (16, 8)
STAGES = 2
FULL = 8
WHOLE = 4
GROUPS = 5
MESH = pl.DeviceIdType.MESH


def norm(x):
    center = x - jnp.mean(x, axis=0, keepdims=True)
    return center * lax.rsqrt(jnp.mean(center * center, axis=0, keepdims=True) + EPS)


def sigmoid(x):
    return 0.5 * jnp.tanh(0.5 * x) + 0.5


def dot(a, b):
    return jnp.dot(a, b, preferred_element_type=F32)


def turned(w_ref):
    return w_ref[...].astype(F32).T.astype(BF16)


def exchange(parts):
    group = lax.broadcasted_iota(jnp.int32, parts[0].shape, 1) // RUN
    parts = list(parts)
    for bit in (1, 2, 4):
        chosen = (group // bit) % 2 == 1
        for i in range(8):
            if i & bit:
                continue
            low, high = parts[i], parts[i + bit]
            parts[i] = jnp.where(chosen, pltpu.roll(high, RUN * bit, 1), low)
            parts[i + bit] = jnp.where(chosen, high, pltpu.roll(low, LANES - RUN * bit, 1))
    return parts


def coordinates():
    row, col = lax.axis_index("row"), lax.axis_index("col")
    return row * 2 + (col // 2) % 2, (col // 4) * 2 + col % 2


def device(place):
    plane, x = place
    return plane // 2, (x // 2) * 4 + (plane % 2) * 2 + x % 2


def loop(n, f, unroll=1):
    def step(i, _):
        f(i)
        return 0

    lax.fori_loop(0, n, step, 0, unroll=unroll)


def along(ref, axis, at):
    return ref.at[(slice(None),) * axis + (at,)]


class Move:
    def __init__(self, me, buffers, index, send, receive, local):
        self.me, self.buffers, self.index = me, buffers, index
        self.send, self.receive, self.local = send, receive, local

    def parts(self, group, stage):
        axis = (stage + 1 + group) % 2
        source, target = [
            whole.at[group] if group < WHOLE else last.at[0]
            for whole, last in self.buffers[stage : stage + 2]
        ]
        return axis, source, target, (self.index, group, stage)

    def start(self, group, stage):
        axis, source, target, at = self.parts(group, stage)
        here = self.me[axis]
        for step in range(1, SIZES[axis]):
            there = (here + step) % SIZES[axis]
            place = list(self.me)
            place[axis] = there
            pltpu.make_async_remote_copy(
                src_ref=along(source, axis, there),
                dst_ref=along(target, axis, here),
                send_sem=self.send.at[at],
                recv_sem=self.receive.at[at],
                device_id=device(place),
                device_id_type=MESH,
            ).start()
        pltpu.make_async_copy(
            along(source, axis, here), along(target, axis, here), self.local.at[at]
        ).start()

    def arrive(self, group, stage):
        axis, source, target, at = self.parts(group, stage)
        most = along(target, axis, slice(1, SIZES[axis]))
        pltpu.make_async_copy(most, most, self.receive.at[at]).wait()
        one = along(target, axis, self.me[axis])
        pltpu.make_async_copy(one, one, self.local.at[at]).wait()

    def sent(self):
        for group in range(GROUPS):
            for stage in range(STAGES):
                axis, source, target, at = self.parts(group, stage)
                most = along(source, axis, slice(1, SIZES[axis]))
                pltpu.make_async_copy(most, most, self.send.at[at]).wait()

    def advance(self):
        for group in range(GROUPS):
            self.arrive(group, 0)
            self.start(group, 1)

    def at_group(self, group, act):
        if isinstance(group, int):
            act(group)
            return
        for one in range(GROUPS):
            pl.when(group == one)(functools.partial(act, one))

    def begin(self, group):
        self.at_group(group, lambda one: self.start(one, 0))

    def end(self, group):
        self.at_group(group, lambda one: self.arrive(one, 1))


def spans(rows):
    return [(n * FULL, n * FULL + FULL // 2) for n in range(rows // FULL)]


def put(flat, buffers, group, short):
    whole, last = buffers
    planes, places, rows = whole.shape[1:4]

    def one(plane):
        block = flat[pl.ds(pl.multiple_of(plane * places * rows, 8), places * rows), :]
        for x in range(places):
            part = block[x * rows : (x + 1) * rows]
            if short:
                part = jnp.concatenate([part[i:j] for i, j in spans(rows)], axis=0)
                last[0, plane, x] = part.astype(BF16)
            else:
                whole[group, plane, x] = part.astype(BF16)

    loop(planes, one, 2)


def take(buffers, flat, group, short):
    whole, last = buffers
    planes, places, rows = whole.shape[1:4]

    def one(plane):
        first = pl.multiple_of(plane * places * rows, 8)
        if short:
            for x in range(places):
                part = last[0, plane, x].astype(F32)
                for n, (i, j) in enumerate(spans(rows)):
                    flat[pl.ds(first + (x * rows + i), j - i), :] = part[n * (j - i) : (n + 1) * (j - i)]
        else:
            block = [whole[group, plane, x].astype(F32) for x in range(places)]
            flat[pl.ds(first, places * rows), :] = jnp.concatenate(block, axis=0)

    loop(planes, one, 2)


def kernel(
    x_ref, mask_ref, ab1_ref, gate1_ref, z1_ref, ab2_ref, gate2_ref, z2_ref, up_ref, down_ref,
    out_ref,
    current_ref, gating_ref, flat_two, flat_one, mats, left_t, sums, *rest,
):
    n_row, n_col = 8, 16
    rows, cols, channels = x_ref.shape
    n_a, n_b = rows // SUB, cols // RUN
    tile = n_row * n_a
    tiles = 2 * n_b
    half = FULL // 2
    me = coordinates()
    buffers, (send, receive, local) = rest[:-3], rest[-3:]
    moves = []
    for index in range(4):
        mine = buffers[index * 6 : index * 6 + 6]
        pairs = [mine[i : i + 2] for i in range(0, 6, 2)]
        moves.append(Move(me, pairs, index, send, receive, local))

    barrier = pltpu.get_barrier_semaphore()
    for axis in range(len(SIZES)):
        for step in range(1, SIZES[axis]):
            place = list(me)
            place[axis] = (me[axis] + step) % SIZES[axis]
            pl.semaphore_signal(barrier, inc=1, device_id=device(place), device_id_type=MESH)

    def each_group(f):
        loop(WHOLE, lambda group: f(group, FULL))
        f(WHOLE, half)

    def lanes_of(group, count):
        return pl.ds(pl.multiple_of(group * (FULL * LANES), LANES), count * LANES)

    def blocks_of(group, count):
        found = []
        for i in range(count // half):
            number = group * 2 + i
            b, a = number // (n_a // half), number % (n_a // half)
            found.append(
                (
                    pl.ds(pl.multiple_of(a * (half * SUB), half * SUB), half * SUB),
                    pl.ds(pl.multiple_of(b * RUN, RUN), RUN),
                )
            )
        return found

    def emit(group, count, current, ab, gate, move):
        normed = norm(current).astype(BF16)
        hidden = ab.shape[0] // 4
        mask = jnp.concatenate(
            [mask_ref[pl.ds(group * FULL + j, 1), :] for j in range(count)], axis=1
        )
        p = dot(ab, normed)
        left = mask * sigmoid(p[hidden : 2 * hidden]) * p[:hidden]
        right = mask * sigmoid(p[3 * hidden :]) * p[2 * hidden : 3 * hidden]
        for j in range(count):
            lanes = slice(j * LANES, (j + 1) * LANES)
            flat_two[pl.ds(j, hidden, stride=2 * FULL), :] = left[:, lanes]
            flat_two[pl.ds(FULL + j, hidden, stride=2 * FULL), :] = right[:, lanes]
        gating_ref[:, lanes_of(group, count)] = sigmoid(dot(gate, normed))
        put(flat_two, move.buffers[0], group, count < FULL)

    def finish(group, count, z, move):
        take(move.buffers[STAGES], flat_one, group, count < FULL)
        triangle = jnp.concatenate(
            [flat_one[pl.ds(j, channels, stride=FULL), :] for j in range(count)], axis=1
        )
        here = lanes_of(group, count)
        update = gating_ref[:, here] * dot(z, norm(triangle).astype(BF16))
        return (current_ref[:, here].astype(F32) + update).astype(BF16)

    def place_of(a, a_lo):
        t = a // (n_a // 2)
        rest = a % (n_a // 2)
        return t * (n_b * LANES) + (rest // 2) * LANES + (rest % 2) * SUB + a_lo

    def place_at(c):
        return (c % 2) * 8 + (c // 2) * 2

    def pairs_of(group, i):
        for u in range(2):
            inside = i * 4 + u * 2
            number = group * (FULL // 2) + i * 2 + u
            yield inside, number // (n_a // 2), (number % (n_a // 2)) * 2

    def triangle(outgoing, inward, outward):
        def enter(group):
            inward.end(group)
            pl.when(group < WHOLE)(
                lambda: take(inward.buffers[STAGES], flat_two, group, False)
            )
            pl.when(group == WHOLE)(
                lambda: take(inward.buffers[STAGES], flat_two, group, True)
            )
            for operand in range(2):
                scatter = outgoing and operand == 1

                def some(i, operand=operand, scatter=scatter):
                    for inside, b, a in pairs_of(group, i):
                        for parity in range(2):
                            column = parity * n_b + b
                            parts = []
                            for c in range(8):
                                pieces = [
                                    flat_two[
                                        pl.ds(
                                            (place_at(c) + parity) * 2 * FULL
                                            + operand * FULL + inside + odd,
                                            n_row,
                                            stride=n_col * 2 * FULL,
                                        ),
                                        :,
                                    ]
                                    for odd in range(2)
                                ]
                                parts.append(jnp.concatenate(pieces, axis=0).astype(BF16))
                            parts = exchange(parts)
                            for a_lo in range(8):
                                if scatter:
                                    wide = parts[a_lo].astype(F32)
                                    for odd in range(2):
                                        start = place_of(a + odd, a_lo)
                                        sums[column, pl.ds(start, n_row, stride=RUN), :] = (
                                            wide[odd * n_row : (odd + 1) * n_row]
                                        )
                                else:
                                    start = pl.multiple_of(a_lo * tile + a * n_row, 16)
                                    mats[operand, column, pl.ds(start, 16), :] = parts[a_lo]

                lax.fori_loop(0, 2 - group // WHOLE, lambda i, _: (some(i), 0)[1], 0)

            def settle(b):
                for column in (b, n_b + b):
                    if outgoing:
                        mats[1, column] = sums[column].astype(BF16)
                    else:
                        left_t[column] = mats[0, column].T

            for b, complete in ((0, 1), (1, 2), (2, 4)):
                pl.when(group == complete)(functools.partial(settle, b))

        loop(GROUPS, enter)

        def multiply(b):
            if outgoing:
                whole = jnp.concatenate([mats[0, n] for n in range(tiles)], axis=1)
                both = [
                    jnp.concatenate(
                        [mats[1, k, column * LANES : (column + 1) * LANES] for k in range(tiles)],
                        axis=1,
                    )
                    for column in (b, n_b + b)
                ]
                right = jnp.concatenate(both, axis=0)
                form = (((1,), (1,)), ((), ()))
            else:
                whole = jnp.concatenate([left_t[n] for n in range(tiles)], axis=0)
                right = jnp.concatenate([mats[1, b], mats[1, n_b + b]], axis=1)
                form = (((1,), (0,)), ((), ()))
            total = lax.dot_general(whole, right, form, preferred_element_type=F32)
            sums[b] = total[:, :LANES]
            sums[n_b + b] = total[:, LANES:]

        def leave(group):
            for b, needed in ((0, 0), (1, 1), (2, 3)):
                pl.when(group == needed)(functools.partial(multiply, b))

            def some(i):
                for inside, b, a in pairs_of(group, i):
                    for parity in range(2):
                        column = parity * n_b + b
                        parts = []
                        for a_lo in range(8):
                            if outgoing:
                                start = pl.multiple_of(a_lo * tile + a * n_row, 16)
                                value = sums[column, pl.ds(start, 16), :]
                            else:
                                value = jnp.concatenate(
                                    [
                                        sums[
                                            column,
                                            pl.ds(place_of(a + odd, a_lo), n_row, stride=RUN),
                                            :,
                                        ]
                                        for odd in range(2)
                                    ],
                                    axis=0,
                                )
                            parts.append(value.astype(BF16))
                        for c, part in enumerate(exchange(parts)):
                            wide = part.astype(F32)
                            for odd in range(2):
                                flat_one[
                                    pl.ds(
                                        (place_at(c) + parity) * FULL + inside + odd,
                                        n_row,
                                        stride=n_col * FULL,
                                    ),
                                    :,
                                ] = wide[odd * n_row : (odd + 1) * n_row]

            lax.fori_loop(0, 2 - group // WHOLE, lambda i, _: (some(i), 0)[1], 0)
            pl.when(group < WHOLE)(lambda: put(flat_one, outward.buffers[0], group, False))
            pl.when(group == WHOLE)(lambda: put(flat_one, outward.buffers[0], group, True))
            outward.begin(group)

        loop(GROUPS, leave)

    ab, gate = turned(ab1_ref), turned(gate1_ref)

    def first(group, count):
        block = [x_ref[a, b, :].reshape(half * LANES, channels) for a, b in blocks_of(group, count)]
        current = jnp.concatenate(block, axis=0).astype(F32).T
        current_ref[:, lanes_of(group, count)] = current.astype(BF16)
        emit(group, count, current, ab, gate, moves[0])
        if not isinstance(group, int):
            pl.when(group == 0)(
                lambda: pl.semaphore_wait(barrier, sum(SIZES) - len(SIZES))
            )
        moves[0].begin(group)

    each_group(first)
    moves[0].advance()
    triangle(True, moves[0], moves[1])

    z, ab2, gate2 = turned(z1_ref), turned(ab2_ref), turned(gate2_ref)
    moves[1].advance()

    def middle(group, count):
        moves[1].end(group)
        current = finish(group, count, z, moves[1])
        current_ref[:, lanes_of(group, count)] = current
        emit(group, count, current.astype(F32), ab2, gate2, moves[2])
        moves[2].begin(group)

    each_group(middle)
    moves[2].advance()
    triangle(False, moves[2], moves[3])

    z2, up, down = turned(z2_ref), turned(up_ref), turned(down_ref)
    moves[3].advance()

    def last(group, count):
        moves[3].end(group)
        current = finish(group, count, z2, moves[3]).astype(F32)
        expanded = jnp.maximum(dot(up, norm(current).astype(BF16)), 0.0).astype(BF16)
        result = (current + dot(down, expanded)).T.astype(out_ref.dtype)
        for i, (a, b) in enumerate(blocks_of(group, count)):
            part = result[i * half * LANES : (i + 1) * half * LANES]
            out_ref[a, b, :] = part.reshape(half * SUB, RUN, channels)

    each_group(last)
    for move in moves:
        move.sent()


def body(
    pair,
    residue_mask,
    out_ab_weight,
    out_gate_weight,
    out_z_weight,
    in_ab_weight,
    in_gate_weight,
    in_z_weight,
    trans_up,
    trans_down,
):
    rows, cols, channels = pair.shape
    n_a, n_b = rows // SUB, cols // RUN
    chunks = n_a * n_b
    size = 8 * rows
    present = residue_mask.astype(F32)
    mask_rows = lax.dynamic_slice_in_dim(present, lax.axis_index("row") * rows, rows)
    mask_cols = lax.dynamic_slice_in_dim(present, lax.axis_index("col") * cols, cols)
    mask = (
        mask_rows.reshape(1, n_a, SUB, 1) * mask_cols.reshape(n_b, 1, 1, RUN)
    ).reshape(chunks, LANES)
    vmem = pl.BlockSpec(memory_space=pltpu.VMEM)
    buffers = []
    for rows_each in (2 * FULL, FULL, 2 * FULL, FULL):
        for _ in range(STAGES + 1):
            buffers.append(pltpu.VMEM((WHOLE,) + SIZES + (rows_each, LANES), BF16))
            buffers.append(pltpu.VMEM((1,) + SIZES + (rows_each // 2, LANES), BF16))
    return pl.pallas_call(
        kernel,
        out_shape=jax.ShapeDtypeStruct(pair.shape, pair.dtype),
        in_specs=[vmem] * 10,
        out_specs=vmem,
        scratch_shapes=[
            pltpu.VMEM((channels, chunks * LANES), BF16),
            pltpu.VMEM((channels, chunks * LANES), F32),
            pltpu.VMEM((channels * 2 * FULL, LANES), F32),
            pltpu.VMEM((channels * FULL, LANES), F32),
            pltpu.VMEM((2, size // LANES, size, LANES), BF16),
            pltpu.VMEM((size // LANES, LANES, size), BF16),
            pltpu.VMEM((size // LANES, size, LANES), F32),
            *buffers,
            pltpu.SemaphoreType.DMA((4, GROUPS, STAGES)),
            pltpu.SemaphoreType.DMA((4, GROUPS, STAGES)),
            pltpu.SemaphoreType.DMA((4, GROUPS, STAGES)),
        ],
        compiler_params=pltpu.CompilerParams(
            collective_id=0, has_side_effects=True, vmem_limit_bytes=60 << 20
        ),
    )(
        pair, mask, out_ab_weight, out_gate_weight, out_z_weight, in_ab_weight, in_gate_weight,
        in_z_weight, trans_up, trans_down,
    )


def solution(mesh):
    placed = (P("row", "col", None), P(), P(), P(), P(), P(), P(), P(), P(), P())
    return jax.shard_map(
        body, mesh=mesh, in_specs=placed, out_specs=P("row", "col", None), check_vma=False
    )
```

time: 131 us -> 117 us (0.89)
  Pallas kernels: 126 us -> 112 us
    pallas_call x1, Pallas kernels: 126 us -> 112 us  [body(): pl.pallas_call(kernel, out_shape=jax.ShapeDtypeStruct(pair.shape, pair.dt...]
where the time goes in v6:
time: 117 us; the launch traced here: 116 us
  Pallas kernels  112 us (96%)
  local copies, waits for them, and re-layouts  3.38 us (3%)
    pallas_call x1, Pallas kernels, body(): pl.pallas_call(kernel, out_shape=jax.ShapeDtypeStruct(pair.shape, pair.dt...  112 us
    unnamed x1, local copies, waits for them, and re-layouts  2.36 us

profile of v6, /device:TPU:1, one launch (start us, length us, event | category | flops | bytes accessed | tf_op | source)
XLA Modules:
  0.0 116.0 jit_solution(3910014465449465306)
XLA Ops:
  0.0 0.7 convert_element_type.3
  0.7 0.1 dynamic_slice.7
  0.8 0.1 dynamic_slice.6
  0.8 0.1 mul.31
  0.9 0.1 mul.28
  1.0 0.1 broadcast_multiply_fusion
  1.1 0.7 mul.34.mask_ref
  1.8 111.8 %shard_map.100 = bf16[96,48,128]{2,1,0:T(8,128)(2,1)} custom-call(bf16[96,48,128]{2,1,0:T(8,128)(2,1)} %x_ref.1, f32[36,128]{1,0:T(8,128)} %mul.34.mask_ref, bf16[128,512]{1,0:T(8,128)(2,1)} %ab1_ref.1, bf16[128,128]{1,0:T(8,128)(2,1)} %gate1_ref.1, bf16[128,128]{1,0:T(8,128)(2,1)} %z1_ref.1, bf16[128,512]{1,0:T(8,128)(2,1)} %ab2_ref.1, ...), custom_call_target="tpu_custom_call" | custom-call | tf_op jit(solution)/shard_map/pallas_call | solution.py:466
  113.6 2.4 %copy.12 = bf16[96,48,128]{2,1,0:T(8,128)(2,1)} copy(bf16[96,48,128]{2,1,0:T(8,128)(2,1)} %shard_map.100) | data formatting | bytes 2359296

commit v7 on v6

--- a/solution.py
+++ b/solution.py
@@ -81,7 +81,7 @@
         self.send, self.receive, self.local = send, receive, local
 
     def parts(self, group, stage):
-        axis = (stage + 1 + group) % 2
+        axis = (stage + group + self.index) % 2
         source, target = [
             whole.at[group] if group < WHOLE else last.at[0]
             for whole, last in self.buffers[stage : stage + 2]
@@ -91,7 +91,7 @@
     def start(self, group, stage):
         axis, source, target, at = self.parts(group, stage)
         here = self.me[axis]
-        for step in range(1, SIZES[axis]):
+        for step in reversed(range(1, SIZES[axis])):
             there = (here + step) % SIZES[axis]
             place = list(self.me)
             place[axis] = there
@@ -182,7 +182,7 @@
 def kernel(
     x_ref, mask_ref, ab1_ref, gate1_ref, z1_ref, ab2_ref, gate2_ref, z2_ref, up_ref, down_ref,
     out_ref,
-    current_ref, gating_ref, flat_two, flat_one, mats, left_t, sums, *rest,
+    current_ref, gating_ref, flat_two, flat_one, mats, left_t, sums, mask_rows, mask_cols, *rest,
 ):
     n_row, n_col = 8, 16
     rows, cols, channels = x_ref.shape
@@ -209,6 +209,28 @@
         loop(WHOLE, lambda group: f(group, FULL))
         f(WHOLE, half)
 
+    present = mask_ref[...].reshape(1, n_row * rows).astype(F32)
+    size = present.shape[1]
+    lane = lax.broadcasted_iota(jnp.int32, (size, LANES), 1)
+    residue = lax.broadcasted_iota(jnp.int32, (size, LANES), 0)
+    for target, begin, step, chosen in (
+        (mask_rows, lax.axis_index("row") * rows, SUB, lane // RUN),
+        (mask_cols, lax.axis_index("col") * cols, RUN, lane % RUN),
+    ):
+        line = lax.broadcasted_iota(jnp.int32, (target.shape[0], size), 0)
+        index = lax.broadcasted_iota(jnp.int32, (target.shape[0], size), 1)
+        mine = jnp.where(index // step - begin // step == line, present, 0.0).astype(BF16)
+        target[...] = dot(mine, jnp.where(residue % step == chosen, 1.0, 0.0).astype(BF16))
+
+    def mask_of(group, count):
+        found = []
+        for j in range(count):
+            chunk = group * FULL + j
+            found.append(
+                mask_rows[pl.ds(chunk % n_a, 1), :] * mask_cols[pl.ds(chunk // n_a, 1), :]
+            )
+        return jnp.concatenate(found, axis=1)
+
     def lanes_of(group, count):
         return pl.ds(pl.multiple_of(group * (FULL * LANES), LANES), count * LANES)
 
@@ -228,9 +250,7 @@
     def emit(group, count, current, ab, gate, move):
         normed = norm(current).astype(BF16)
         hidden = ab.shape[0] // 4
-        mask = jnp.concatenate(
-            [mask_ref[pl.ds(group * FULL + j, 1), :] for j in range(count)], axis=1
-        )
+        mask = mask_of(group, count)
         p = dot(ab, normed)
         left = mask * sigmoid(p[hidden : 2 * hidden]) * p[:hidden]
         right = mask * sigmoid(p[3 * hidden :]) * p[2 * hidden : 3 * hidden]
@@ -451,12 +471,6 @@
     n_a, n_b = rows // SUB, cols // RUN
     chunks = n_a * n_b
     size = 8 * rows
-    present = residue_mask.astype(F32)
-    mask_rows = lax.dynamic_slice_in_dim(present, lax.axis_index("row") * rows, rows)
-    mask_cols = lax.dynamic_slice_in_dim(present, lax.axis_index("col") * cols, cols)
-    mask = (
-        mask_rows.reshape(1, n_a, SUB, 1) * mask_cols.reshape(n_b, 1, 1, RUN)
-    ).reshape(chunks, LANES)
     vmem = pl.BlockSpec(memory_space=pltpu.VMEM)
     buffers = []
     for rows_each in (2 * FULL, FULL, 2 * FULL, FULL):
@@ -476,6 +490,8 @@
             pltpu.VMEM((2, size // LANES, size, LANES), BF16),
             pltpu.VMEM((size // LANES, LANES, size), BF16),
             pltpu.VMEM((size // LANES, size, LANES), F32),
+            pltpu.VMEM((16, LANES), F32),
+            pltpu.VMEM((8, LANES), F32),
             *buffers,
             pltpu.SemaphoreType.DMA((4, GROUPS, STAGES)),
             pltpu.SemaphoreType.DMA((4, GROUPS, STAGES)),
@@ -485,7 +501,7 @@
             collective_id=0, has_side_effects=True, vmem_limit_bytes=60 << 20
         ),
     )(
-        pair, mask, out_ab_weight, out_gate_weight, out_z_weight, in_ab_weight, in_gate_weight,
+        pair, residue_mask, out_ab_weight, out_gate_weight, out_z_weight, in_ab_weight, in_gate_weight,
         in_z_weight, trans_up, trans_down,
     )
 

time: 117 us -> 112 us (0.957)
  Pallas kernels: 112 us -> 109 us
    pallas_call x1, Pallas kernels: 112 us -> 109 us  [body(): pl.pallas_call(kernel, out_shape=jax.ShapeDtypeStruct(pair.shape, pair.dt...]
where the time goes in v7:
time: 112 us
  Pallas kernels  109 us (97%)
  local copies, waits for them, and re-layouts  2.36 us (2%)
    pallas_call x1, Pallas kernels, body(): pl.pallas_call(kernel, out_shape=jax.ShapeDtypeStruct(pair.shape, pair.dt...  109 us
    unnamed x1, local copies, waits for them, and re-layouts  2.36 us

profile of v7, /device:TPU:1, one launch (start us, length us, event | category | flops | bytes accessed | tf_op | source)
XLA Modules:
  0.0 111.5 jit_solution(1829762616320249175)
XLA Ops:
  0.0 109.2 %shard_map.100 = bf16[96,48,128]{2,1,0:T(8,128)(2,1)} custom-call(bf16[96,48,128]{2,1,0:T(8,128)(2,1)} %x_ref.1, s32[768]{0:T(1024)} %mask_ref.1, bf16[128,512]{1,0:T(8,128)(2,1)} %ab1_ref.1, bf16[128,128]{1,0:T(8,128)(2,1)} %gate1_ref.1, bf16[128,128]{1,0:T(8,128)(2,1)} %z1_ref.1, bf16[128,512]{1,0:T(8,128)(2,1)} %ab2_ref.1, bf16[128,128]{1,0:T(8,128)(2,1)} %gate2_ref.1, ...), custom_call_target="tpu_custom_call" | custom-call | tf_op jit(solution)/shard_map/pallas_call | solution.py:480
  109.2 2.4 %copy.12 = bf16[96,48,128]{2,1,0:T(8,128)(2,1)} copy(bf16[96,48,128]{2,1,0:T(8,128)(2,1)} %shard_map.100) | data formatting | bytes 2359296

commit v8 on v7

--- a/solution.py
+++ b/solution.py
@@ -158,7 +158,7 @@
             else:
                 whole[group, plane, x] = part.astype(BF16)
 
-    loop(planes, one, 2)
+    loop(planes, one, 4)
 
 
 def take(buffers, flat, group, short):
@@ -176,7 +176,7 @@
             block = [whole[group, plane, x].astype(F32) for x in range(places)]
             flat[pl.ds(first, places * rows), :] = jnp.concatenate(block, axis=0)
 
-    loop(planes, one, 2)
+    loop(planes, one, 4)
 
 
 def kernel(
@@ -439,6 +439,8 @@
     triangle(False, moves[2], moves[3])
 
     z2, up, down = turned(z2_ref), turned(up_ref), turned(down_ref)
+    for move in moves[:3]:
+        move.sent()
     moves[3].advance()
 
     def last(group, count):
@@ -451,8 +453,7 @@
             out_ref[a, b, :] = part.reshape(half * SUB, RUN, channels)
 
     each_group(last)
-    for move in moves:
-        move.sent()
+    moves[3].sent()
 
 
 def body(

time: 112 us -> 112 us (level)
  no operation moved by 1% of the time
where the time goes in v8:
time: 112 us
  Pallas kernels  109 us (97%)
  local copies, waits for them, and re-layouts  2.36 us (2%)
    pallas_call x1, Pallas kernels, body(): pl.pallas_call(kernel, out_shape=jax.ShapeDtypeStruct(pair.shape, pair.dt...  109 us
    unnamed x1, local copies, waits for them, and re-layouts  2.36 us

profile of v8, /device:TPU:1, one launch (start us, length us, event | category | flops | bytes accessed | tf_op | source)
XLA Modules:
  0.0 111.6 jit_solution(2784692850819550113)
XLA Ops:
  0.0 109.2 %shard_map.100 = bf16[96,48,128]{2,1,0:T(8,128)(2,1)} custom-call(bf16[96,48,128]{2,1,0:T(8,128)(2,1)} %x_ref.1, s32[768]{0:T(1024)} %mask_ref.1, bf16[128,512]{1,0:T(8,128)(2,1)} %ab1_ref.1, bf16[128,128]{1,0:T(8,128)(2,1)} %gate1_ref.1, bf16[128,128]{1,0:T(8,128)(2,1)} %z1_ref.1, bf16[128,512]{1,0:T(8,128)(2,1)} %ab2_ref.1, bf16[128,128]{1,0:T(8,128)(2,1)} %gate2_ref.1, ...), custom_call_target="tpu_custom_call" | custom-call | tf_op jit(solution)/shard_map/pallas_call | solution.py:481
  109.2 2.4 %copy.12 = bf16[96,48,128]{2,1,0:T(8,128)(2,1)} copy(bf16[96,48,128]{2,1,0:T(8,128)(2,1)} %shard_map.100) | data formatting | bytes 2359296
